TPU v7x, 32 devices: a whole 2x2x4 slice. The times are simulated.
32 devices in a mesh: dp: 4 (over z), ctx: 8 (over y, x, core).
Axes of the slice: x: 2, y: 2, z: 4, core: 2. Of those that a mesh axis runs over, the one named last changes fastest.
Arguments:
- hidden_in: bfloat16 [4, 1024, 768], P('dp', 'ctx'), may hold values from -6 to 6
- segment_ids: int32 [4, 1024], P('dp', 'ctx'), may hold values from 0 to 4, as said below
- w_qkv: bfloat16 [768, 2304], P('dp'), may hold values from -0.21875 to 0.21875
- w_out: bfloat16 [768, 768], P('dp'), may hold values from -4 to 4
- w_in: bfloat16 [768, 2304], P('dp'), may hold values from -0.21875 to 0.21875
- w_down: bfloat16 [1152, 768], P('dp'), may hold values from -0.1875 to 0.1875
- gain_attn: bfloat16 [768], P('dp'), may hold values from 0.5 to 1.5
- gain_mlp: bfloat16 [768], P('dp'), may hold values from 0.5 to 1.5
- cotangent: bfloat16 [4, 1024, 768], P('dp', 'ctx'), may hold values from -6 to 6
Outputs:
- output: bfloat16 [4, 1024, 768], P('dp', 'ctx')
- grad_input: float32 [4, 1024, 768], P('dp', 'ctx')
- grad_qkv: float32 [768, 2304], P('dp')
- grad_out: float32 [768, 768], P('dp')
- grad_in: float32 [768, 2304], P('dp')
- grad_down: float32 [1152, 768], P('dp')
- grad_gain_attn: float32 [768], P('dp')
- grad_gain_mlp: float32 [768], P('dp')
Inputs may be any that keep to these rules, and one draw needn't show every extreme that they name: `segment_ids`: ids never fall along a sequence; each sequence holds documents 0 to 4; document 2 begins within the first 128 tokens and ends within the last 128; every other document is shorter than 128 tokens.
All inputs are finite; a program needn't handle non-finite values.
Results may differ from a plain program's by a relative error of at most 0.024.
Values may be sent and summed in bfloat16 or wider, within the bound.
A program may use at most 256 MiB of HBM per device.

v0:
```python
import jax
import jax.numpy as jnp
from jax import lax
from jax.sharding import PartitionSpec as P

HEADS = 12


EPSILON = 1e-05
ROPE_THETA = 160000.0
NEGATIVE = -1e30


def layer_norm(values, gain_row):
    average = jnp.mean(values, axis=-1, keepdims=True)
    centred = values - average
    spread = jnp.mean(centred * centred, axis=-1, keepdims=True)
    return centred * lax.rsqrt(spread + EPSILON) * gain_row


def rope_tables(first_row, row_count, head_size):
    position = (first_row + jnp.arange(row_count, dtype=jnp.int32)).astype(jnp.float32)
    frequency = ROPE_THETA ** (-jnp.arange(0, head_size, 2, dtype=jnp.float32) / head_size)
    angles = position[:, None] * frequency[None, :]
    angles = jnp.concatenate([angles, angles], axis=-1)
    return (jnp.cos(angles)[:, None, :], jnp.sin(angles)[:, None, :])


def rotary(values, cosines, sines):
    half_size = values.shape[-1] // 2
    turned = jnp.concatenate([-values[..., half_size:], values[..., :half_size]], axis=-1)
    return values * cosines + turned * sines


def rotary_back(grads, cosines, sines):
    half_size = grads.shape[-1] // 2
    shifted = grads * sines
    return grads * cosines + jnp.concatenate(
        [shifted[..., half_size:], -shifted[..., :half_size]], axis=-1
    )


def geglu(gate_in, gate_up):
    return jax.nn.gelu(gate_in, approximate=False) * gate_up


def contract_rows(left_side, right_side):
    return lax.dot_general(
        left_side, right_side, (((0,), (0,)), ((), ())), preferred_element_type=jnp.float32
    )


def contract_cols(left_side, right_side):
    return lax.dot_general(
        left_side, right_side, (((1,), (1,)), ((), ())), preferred_element_type=jnp.float32
    )


def local(hidden_in, segment_ids, w_qkv, w_out, w_in, w_down, gain_attn, gain_mlp, cotangent):
    local_rows = hidden_in.shape[1]
    model_width = hidden_in.shape[2]
    head_count = HEADS
    head_size = model_width // head_count
    score_scale = head_size ** (-0.5)
    head_shape = (local_rows, head_count, head_size)
    shards = (w_qkv, w_out, w_in, w_down, gain_attn, gain_mlp)
    qkv_full, out_full, in_full, down_full, attn_scale, mlp_scale = (
        lax.all_gather(shards[0], "dp", axis=0, tiled=True),
        lax.all_gather(shards[1], "dp", axis=0, tiled=True),
        lax.all_gather(shards[2], "dp", axis=0, tiled=True),
        lax.all_gather(shards[3], "dp", axis=0, tiled=True),
        lax.all_gather(shards[4], "dp", axis=0, tiled=True),
        lax.all_gather(shards[5], "dp", axis=0, tiled=True),
    )
    hidden_units = in_full.shape[1] // 2
    source = hidden_in[0].astype(jnp.float32)
    own_ids = segment_ids[0]
    cosines, sines = rope_tables(lax.axis_index("ctx") * local_rows, local_rows, head_size)
    normed_one = layer_norm(source, attn_scale.astype(jnp.float32)).astype(jnp.bfloat16)
    projected = jnp.dot(normed_one, qkv_full, preferred_element_type=jnp.float32)
    queries = rotary(projected[:, :model_width].reshape(head_shape), cosines, sines).astype(
        jnp.bfloat16
    )
    own_keys = rotary(
        projected[:, model_width : 2 * model_width].reshape(head_shape), cosines, sines
    ).astype(jnp.bfloat16)
    value_flat = projected[:, 2 * model_width :].astype(jnp.bfloat16)
    own_values = value_flat.reshape(head_shape)
    key_flat = own_keys.reshape(local_rows, model_width)
    query_flat = queries.reshape(local_rows, model_width)
    highest = jnp.full((head_count, local_rows), NEGATIVE, jnp.float32)
    block_keys = lax.all_gather(key_flat, "ctx", axis=0, tiled=True)
    block_values = lax.all_gather(value_flat, "ctx", axis=0, tiled=True)
    block_ids = lax.all_gather(own_ids, "ctx", axis=0, tiled=True)
    piece_rows = block_keys.shape[0]
    scores = (
        jnp.einsum(
            "qhe,khe->hqk",
            queries,
            block_keys.reshape(piece_rows, head_count, head_size),
            preferred_element_type=jnp.float32,
        )
        * score_scale
    )
    allowed = (own_ids[:, None] == block_ids[None, :])[None]
    scores = jnp.where(allowed, scores, NEGATIVE)
    raised = jnp.maximum(highest, jnp.max(scores, axis=-1))
    weights = jnp.where(allowed, jnp.exp(scores - raised[..., None]), 0.0)
    row_total = jnp.sum(weights, axis=-1)
    update = jnp.einsum(
        "hqk,khe->qhe",
        weights.astype(jnp.bfloat16),
        block_values.reshape(piece_rows, head_count, head_size),
        preferred_element_type=jnp.float32,
    )
    summed = update
    highest, row_total, summed = (raised, row_total, summed)
    attention = summed / jnp.transpose(row_total)[:, :, None]
    log_total = highest + jnp.log(row_total)
    attended = attention.reshape(local_rows, model_width).astype(jnp.bfloat16)
    middle = source + jnp.dot(attended, out_full, preferred_element_type=jnp.float32)
    normed_two = layer_norm(middle, mlp_scale.astype(jnp.float32)).astype(jnp.bfloat16)
    lifted = jnp.dot(normed_two, in_full, preferred_element_type=jnp.float32)
    gate_in = lifted[:, :hidden_units]
    gate_up = lifted[:, hidden_units:]
    mixed_units = geglu(gate_in, gate_up).astype(jnp.bfloat16)
    result = (middle + jnp.dot(mixed_units, down_full, preferred_element_type=jnp.float32)).astype(
        jnp.bfloat16
    )
    qkv_back, out_back, in_back, down_back, attn_back, mlp_back = (
        lax.all_gather(shards[0], "dp", axis=0, tiled=True),
        lax.all_gather(shards[1], "dp", axis=0, tiled=True),
        lax.all_gather(shards[2], "dp", axis=0, tiled=True),
        lax.all_gather(shards[3], "dp", axis=0, tiled=True),
        lax.all_gather(shards[4], "dp", axis=0, tiled=True),
        lax.all_gather(shards[5], "dp", axis=0, tiled=True),
    )
    upstream = cotangent[0]
    grad_down = contract_rows(mixed_units, upstream)
    grad_mixed = contract_cols(upstream, down_back)
    _, pull_gate = jax.vjp(geglu, gate_in, gate_up)
    grad_gate_in, grad_gate_up = pull_gate(grad_mixed)
    grad_lifted = jnp.concatenate([grad_gate_in, grad_gate_up], axis=1).astype(jnp.bfloat16)
    grad_in = contract_rows(normed_two, grad_lifted)
    grad_normed_two = contract_cols(grad_lifted, in_back)
    _, pull_two = jax.vjp(layer_norm, middle, mlp_back.astype(jnp.float32))
    grad_middle_part, grad_mlp_gain = pull_two(grad_normed_two)
    grad_middle = upstream.astype(jnp.float32) + grad_middle_part
    grad_branch = grad_middle.astype(jnp.bfloat16)
    grad_out = contract_rows(attended, grad_branch)
    grad_attended = contract_cols(grad_branch, out_back).astype(jnp.bfloat16)
    grad_heads = grad_attended.reshape(head_shape)
    products = jnp.transpose(jnp.sum(grad_heads.astype(jnp.float32) * attention, axis=-1))
    all_log, all_products, all_ids = (
        lax.all_gather(log_total, "ctx", axis=1, tiled=True),
        lax.all_gather(products, "ctx", axis=1, tiled=True),
        lax.all_gather(own_ids, "ctx", axis=0, tiled=True),
    )
    block_keys = lax.all_gather(key_flat, "ctx", axis=0, tiled=True)
    block_values = lax.all_gather(value_flat, "ctx", axis=0, tiled=True)
    block_ids = lax.all_gather(own_ids, "ctx", axis=0, tiled=True)
    piece_rows = block_keys.shape[0]
    key_heads = block_keys.reshape(piece_rows, head_count, head_size)
    scores = (
        jnp.einsum("qhe,khe->hqk", queries, key_heads, preferred_element_type=jnp.float32)
        * score_scale
    )
    allowed = (own_ids[:, None] == block_ids[None, :])[None]
    probabilities = jnp.where(allowed, jnp.exp(scores - log_total[..., None]), 0.0)
    grad_probs = jnp.einsum(
        "qhe,khe->hqk",
        grad_heads,
        block_values.reshape(piece_rows, head_count, head_size),
        preferred_element_type=jnp.float32,
    )
    grad_scores = (probabilities * (grad_probs - products[..., None])).astype(jnp.bfloat16)
    grad_queries = score_scale * jnp.einsum(
        "hqk,khe->qhe", grad_scores, key_heads, preferred_element_type=jnp.float32
    )
    block_queries = lax.all_gather(query_flat, "ctx", axis=0, tiled=True)
    block_grads = lax.all_gather(grad_attended, "ctx", axis=0, tiled=True)
    piece_rows = block_queries.shape[0]
    query_heads = block_queries.reshape(piece_rows, head_count, head_size)
    grad_rows = block_grads.reshape(piece_rows, head_count, head_size)
    scores = (
        jnp.einsum("qhe,khe->hqk", query_heads, own_keys, preferred_element_type=jnp.float32)
        * score_scale
    )
    allowed = (all_ids[:, None] == own_ids[None, :])[None]
    probabilities = jnp.where(allowed, jnp.exp(scores - all_log[..., None]), 0.0)
    grad_values = jnp.einsum(
        "hqk,qhe->khe",
        probabilities.astype(jnp.bfloat16),
        grad_rows,
        preferred_element_type=jnp.float32,
    )
    grad_probs = jnp.einsum(
        "qhe,khe->hqk", grad_rows, own_values, preferred_element_type=jnp.float32
    )
    grad_scores = (probabilities * (grad_probs - all_products[..., None])).astype(jnp.bfloat16)
    grad_keys = score_scale * jnp.einsum(
        "hqk,qhe->khe", grad_scores, query_heads, preferred_element_type=jnp.float32
    )
    grad_keys, grad_values = (grad_keys, grad_values)
    grad_projected = jnp.concatenate(
        [
            rotary_back(grad_queries, cosines, sines).reshape(local_rows, model_width),
            rotary_back(grad_keys, cosines, sines).reshape(local_rows, model_width),
            grad_values.reshape(local_rows, model_width),
        ],
        axis=1,
    ).astype(jnp.bfloat16)
    grad_qkv = contract_rows(normed_one, grad_projected)
    grad_normed_one = contract_cols(grad_projected, qkv_back)
    _, pull_one = jax.vjp(layer_norm, source, attn_back.astype(jnp.float32))
    grad_source, grad_attn_gain = pull_one(grad_normed_one)
    grad_input = grad_middle + grad_source
    local_grads = (grad_qkv, grad_out, grad_in, grad_down, grad_attn_gain, grad_mlp_gain)
    shares = (
        lax.psum_scatter(
            local_grads[0].astype(jnp.bfloat16), "dp", scatter_dimension=0, tiled=True
        ).astype(jnp.float32),
        lax.psum_scatter(
            local_grads[1].astype(jnp.bfloat16), "dp", scatter_dimension=0, tiled=True
        ).astype(jnp.float32),
        lax.psum_scatter(
            local_grads[2].astype(jnp.bfloat16), "dp", scatter_dimension=0, tiled=True
        ).astype(jnp.float32),
        lax.psum_scatter(
            local_grads[3].astype(jnp.bfloat16), "dp", scatter_dimension=0, tiled=True
        ).astype(jnp.float32),
        lax.psum_scatter(
            local_grads[4].astype(jnp.bfloat16), "dp", scatter_dimension=0, tiled=True
        ).astype(jnp.float32),
        lax.psum_scatter(
            local_grads[5].astype(jnp.bfloat16), "dp", scatter_dimension=0, tiled=True
        ).astype(jnp.float32),
    )
    shares = (
        lax.psum(shares[0].astype(jnp.bfloat16), "ctx").astype(jnp.float32),
        lax.psum(shares[1].astype(jnp.bfloat16), "ctx").astype(jnp.float32),
        lax.psum(shares[2].astype(jnp.bfloat16), "ctx").astype(jnp.float32),
        lax.psum(shares[3].astype(jnp.bfloat16), "ctx").astype(jnp.float32),
        lax.psum(shares[4].astype(jnp.bfloat16), "ctx").astype(jnp.float32),
        lax.psum(shares[5].astype(jnp.bfloat16), "ctx").astype(jnp.float32),
    )
    return (
        result[None],
        grad_input[None],
        shares[0],
        shares[1],
        shares[2],
        shares[3],
        shares[4],
        shares[5],
    )


def solution(mesh):
    in_specs = (
        P("dp", "ctx", None),
        P("dp", "ctx"),
        P("dp", None),
        P("dp", None),
        P("dp", None),
        P("dp", None),
        P("dp"),
        P("dp"),
        P("dp", "ctx", None),
    )
    out_specs = (
        P("dp", "ctx", None),
        P("dp", "ctx", None),
        P("dp", None),
        P("dp", None),
        P("dp", None),
        P("dp", None),
        P("dp"),
        P("dp"),
    )
    return jax.shard_map(local, mesh=mesh, in_specs=in_specs, out_specs=out_specs, check_vma=False)
```

profile of v0, /device:TPU:0, one launch (start us, length us, event | category | flops | bytes accessed | tf_op | source)
XLA Modules:
  0.0 630.1 jit_solution(16062213591360769307)
XLA Ops:
  11.6 13.6 %all-reduce.7 = (bf16[768]{0:T(1024)(128)(2,1)S(1)}, bf16[768]{0:T(1024)(128)(2,1)S(1)}) all-reduce(bf16[768]{0:T(1024)(128)(2,1)S(1)} %dynamic-update-slice, bf16[768]{0:T(1024)(128)(2,1)S(1)} %dynamic-update-slice.1), channel_id=1, replica_groups=mesh['dp'=4,'ctx'=8] {'dp'}, use_global_device_ids=true, to_apply=%add | all-reduce | flops 1536 | bytes 6144
  28.5 53.9 %all-gather.10.cloned.1.call-done = bf16[768,2304]{1,0:T(8,128)(2,1)} async-done(((bf16[192,2304]{1,0:T(8,128)(2,1)}), bf16[768,2304]{1,0:T(8,128)(2,1)}) %all-gather.10.cloned.1.call-update) | async-done | bytes 3538960 | tf_op jit(solution)/shard_map/all_gather | solution.py:68
  92.2 8.7 %all-gather = s32[1,1024]{1,0:T(1,128)S(1)} all-gather(s32[1,128]{1,0:T(1,128)S(1)} %copy-done.44), channel_id=2, replica_groups=mesh['dp'=4,'ctx'=8] {'ctx'}, dimensions={1}, use_global_device_ids=true | all-gather | bytes 4608 | tf_op jit(solution)/shard_map/all_gather | solution.py:94
  101.1 12.9 %all-gather.14.cloned.1.call-done = bf16[1024,768]{1,0:T(8,128)(2,1)} async-done(((bf16[128,768]{1,0:T(8,128)(2,1)}), bf16[1024,768]{1,0:T(8,128)(2,1)}) %all-gather.14.cloned.1.call-update) | async-done | bytes 1572880 | tf_op jit(solution)/shard_map/all_gather | solution.py:92
  121.7 19.9 %all-gather.12.cloned.1.call-done = bf16[1024,768]{1,0:T(8,128)(2,1)} async-done(((bf16[128,768]{1,0:T(8,128)(2,1)}), bf16[1024,768]{1,0:T(8,128)(2,1)}) %all-gather.12.cloned.1.call-update) | async-done | bytes 1572880 | tf_op jit(solution)/shard_map/all_gather | solution.py:93
  144.2 5.8 fusion.88
  150.0 23.5 %all-gather.16.cloned.1.call-done = bf16[768,768]{1,0:T(8,128)(2,1)} async-done(((bf16[192,768]{1,0:T(8,128)(2,1)}), bf16[768,768]{1,0:T(8,128)(2,1)}) %all-gather.16.cloned.1.call-update) | async-done | bytes 1179664 | tf_op jit(solution)/shard_map/all_gather | solution.py:69
  176.0 68.1 %all-gather.18.cloned.1.call-done = bf16[768,2304]{1,0:T(8,128)(2,1)} async-done(((bf16[192,2304]{1,0:T(8,128)(2,1)}), bf16[768,2304]{1,0:T(8,128)(2,1)}) %all-gather.18.cloned.1.call-update) | async-done | bytes 3538960 | tf_op jit(solution)/shard_map/all_gather | solution.py:70
  246.8 37.7 %all-gather.20.cloned.1.call-done = bf16[1152,768]{1,0:T(8,128)(2,1)} async-done(((bf16[288,768]{1,0:T(8,128)(2,1)}), bf16[1152,768]{1,0:T(8,128)(2,1)}) %all-gather.20.cloned.1.call-update) | async-done | bytes 1769488 | tf_op jit(solution)/shard_map/all_gather | solution.py:71
  297.0 3.9 convolution_convert_fusion
  304.5 7.0 %all-gather.22.cloned.1.call-done = bf16[1024,768]{1,0:T(8,128)(2,1)} async-done(((bf16[128,768]{1,0:T(8,128)(2,1)}), bf16[1024,768]{1,0:T(8,128)(2,1)}) %all-gather.22.cloned.1.call-update) | async-done | bytes 1572880 | tf_op jit(solution)/shard_map/all_gather | solution.py:180
  314.8 10.1 %all_gather.59 = f32[12,1024]{1,0:T(8,128)} all-gather(f32[12,128]{1,0:T(8,128)S(1)} %log_add_fusion), channel_id=1, replica_groups=mesh['dp'=4,'ctx'=8] {'ctx'}, dimensions={1}, use_global_device_ids=true | all-gather | bytes 55296 | tf_op jit(solution)/shard_map/all_gather | solution.py:155
  326.0 9.1 %all_gather.61 = f32[12,1024]{1,0:T(8,128)} all-gather(f32[12,128]{1,0:T(8,128)S(1)} %bitcast.131), channel_id=1, replica_groups=mesh['dp'=4,'ctx'=8] {'ctx'}, dimensions={1}, use_global_device_ids=true | all-gather | bytes 55296 | tf_op jit(solution)/shard_map/all_gather | solution.py:156
  335.0 5.2 fusion.54
  343.0 9.0 %fusion.17 = f32[128,12,64]{0,2,1:T(8,128)} fusion(bf16[1024,12,64]{0,2,1:T(8,128)(2,1)} %bitcast.105, f32[12,1024,128]{2,1,0:T(8,128)} %fusion.54, f32[12,1024]{1,0:T(8,128)S(1)} %copy-done.30, f32[12,1024]{1,0:T(8,128)S(1)} %copy-done.28, pred[1024,128]{1,0:T(8,128)(4,1)S(1)} %copy-done.26, bf16[1024,12,64]{0,2,1:T(8,128)(2,1)} %bitcast.114, ...), kind=kOutput, calls=%fused_computation.22 | convolution fusion | flops 412090368 | bytes 10256384 | tf_op jit(solution)/shard_map/hqk,qhe->khe/dot_general | solution.py:201
  352.0 7.1 %broadcast_multiply_fusion.1 = (f32[128,12,64]{0,2,1:T(8,128)}, f32[128,12,64]{0,2,1:T(8,128)S(1)}, f32[128,12,64]{0,2,1:T(8,128)}) fusion(f32[128,64]{0,1:T(8,128)} %get-tuple-element.47, f32[128,12,64]{0,2,1:T(8,128)} %fusion.17, bf16[1024,12,64]{0,2,1:T(8,128)(2,1)S(1)} %bitcast.103, f32[12,128,1024]{2,1,0:T(8,128)} %copy-done, ...), kind=kOutput, calls=%fused_computation.102 | convolution fusion | flops 412286976 | bytes 11382784 | tf_op jit(solution)/shard_map/hqk,khe->qhe/dot_general | solution.py:177
  361.6 5.0 fusion.23
  371.4 39.2 %reduce-scatter.11.cloned.1.call-done = bf16[288,768]{1,0:T(8,128)(2,1)} async-done(((bf16[1152,768]{1,0:T(8,128)(2,1)}), bf16[288,768]{1,0:T(8,128)(2,1)}) %reduce-scatter.11.cloned.1.call-update) | async-done | bytes 442384 | tf_op jit(solution)/shard_map/reduce_scatter | solution.py:229
  410.7 67.9 %reduce-scatter.9.cloned.1.call-done = bf16[192,2304]{1,0:T(8,128)(2,1)} async-done(((bf16[768,2304]{1,0:T(8,128)(2,1)}), bf16[192,2304]{1,0:T(8,128)(2,1)}) %reduce-scatter.9.cloned.1.call-update) | async-done | bytes 884752 | tf_op jit(solution)/shard_map/reduce_scatter | solution.py:226
  478.6 69.0 %reduce-scatter.5.cloned.1.call-done = bf16[192,2304]{1,0:T(8,128)(2,1)} async-done(((bf16[768,2304]{1,0:T(8,128)(2,1)}), bf16[192,2304]{1,0:T(8,128)(2,1)}) %reduce-scatter.5.cloned.1.call-update) | async-done | bytes 884752 | tf_op jit(solution)/shard_map/reduce_scatter | solution.py:220
  548.7 3.5 fusion.47
  552.6 10.7 %all-reduce.6 = (bf16[768]{0:T(1024)(128)(2,1)S(1)}, bf16[768]{0:T(1024)(128)(2,1)S(1)}) all-reduce(bf16[768]{0:T(1024)(128)(2,1)S(1)} %get-tuple-element.10, bf16[768]{0:T(1024)(128)(2,1)S(1)} %copy-done.43), channel_id=7, replica_groups=mesh['dp'=4,'ctx'=8] {'dp'}, use_global_device_ids=true, to_apply=%region_20.21.clone | all-reduce | flops 1536 | bytes 6144
  563.5 12.1 %all-reduce.4 = (bf16[192]{0:T(256)(128)(2,1)S(1)}, bf16[192]{0:T(256)(128)(2,1)S(1)}) all-reduce(bf16[192]{0:T(256)(128)(2,1)S(1)} %dynamic-slice.3, bf16[192]{0:T(256)(128)(2,1)S(1)} %dynamic-slice.5), channel_id=1, replica_groups=mesh['dp'=4,'ctx'=8] {'ctx'}, use_global_device_ids=true, to_apply=%region_21.22 | all-reduce | flops 384 | bytes 1536 | tf_op jit(solution)/shard_map/psum | solution.py:244
  577.7 39.2 %all-reduce.10.cloned.1.call-done = (bf16[192,2304]{1,0:T(8,128)(2,1)}, bf16[192,768]{1,0:T(8,128)(2,1)}, bf16[192,2304]{1,0:T(8,128)(2,1)}, bf16[288,768]{1,0:T(8,128)(2,1)}) async-done(((bf16[192,2304]{1,0:T(8,128)(2,1)}, bf16[192,768]{1,0:T(8,128)(2,1)}, bf16[192,2304]{1,0:T(8,128)(2,1)}, bf16[288,768]{1,0:T(8,128)(2,1)}), (bf16[192,2304]{1,0:T(8,128)(2,1)}, bf16[192,768]{1,0:T(8,128)(2,1)}, ...) | async-done | bytes 2506768 | tf_op jit(solution)/shard_map/psum | solution.py:240
  (202 shorter events, 72.0 us)
Async XLA Ops:
  7.2 75.2 %all-gather.10.cloned.1.call-start = ((), (), s32[]{:S(2)}) async-start(), calls=%async_computation.4 | async-start | bytes 4423680 | tf_op jit(solution)/shard_map/all_gather | solution.py:68
  7.9 106.1 %all-gather.14.cloned.1.call-start = ((), (), s32[]{:S(2)}) async-start(), calls=%async_computation.6 | async-start | bytes 1769472 | tf_op jit(solution)/shard_map/all_gather | solution.py:92
  26.1 89.7 %copy-start.22 = (f32[128,64]{0,1:T(8,128)}, f32[128,64]{0,1:T(8,128)S(1)}, u32[]{:S(2)}) copy-start(f32[128,64]{0,1:T(8,128)S(1)} %get-tuple-element.49) | copy-start | bytes 98308
  27.3 57.9 %copy-start.34 = (f32[128]{0:T(128)}, f32[128]{0:T(128)S(1)}, u32[]{:S(2)}) copy-start(f32[128]{0:T(128)S(1)} %broadcast_multiply_fusion.6) | copy-start | bytes 1540
  28.4 56.8 %copy-start.47 = (f32[128]{0:T(128)}, f32[128]{0:T(128)S(1)}, u32[]{:S(2)}) copy-start(f32[128]{0:T(128)S(1)} %fusion.46) | copy-start | bytes 1540
  28.5 56.8 %copy-start.36 = (f32[128]{0:T(128)}, f32[128]{0:T(128)S(1)}, u32[]{:S(2)}) copy-start(f32[128]{0:T(128)S(1)} %fusion.62) | copy-start | bytes 1540
  89.6 52.1 %all-gather.12.cloned.1.call-start = ((), (), s32[]{:S(2)}) async-start(), calls=%async_computation.5 | async-start | bytes 1769472 | tf_op jit(solution)/shard_map/all_gather | solution.py:93
  90.4 83.2 %all-gather.16.cloned.1.call-start = ((), (), s32[]{:S(2)}) async-start(), calls=%async_computation.7 | async-start | bytes 1474560 | tf_op jit(solution)/shard_map/all_gather | solution.py:69
  90.9 153.2 %all-gather.18.cloned.1.call-start = ((), (), s32[]{:S(2)}) async-start(), calls=%async_computation.8 | async-start | bytes 4423680 | tf_op jit(solution)/shard_map/all_gather | solution.py:70
  91.5 192.9 %all-gather.20.cloned.1.call-start = ((), (), s32[]{:S(2)}) async-start(), calls=%async_computation.9 | async-start | bytes 2211840 | tf_op jit(solution)/shard_map/all_gather | solution.py:71
  92.1 219.4 %all-gather.22.cloned.1.call-start = ((), (), s32[]{:S(2)}) async-start(), calls=%async_computation.10 | async-start | bytes 1769472 | tf_op jit(solution)/shard_map/all_gather | solution.py:180
  101.0 43.2 %copy-start.17 = (pred[128,1024]{1,0:T(8,128)(4,1)}, pred[128,1024]{1,0:T(8,128)(4,1)S(1)}, u32[]{:S(2)}) copy-start(pred[128,1024]{1,0:T(8,128)(4,1)S(1)} %broadcast_compare_fusion.1) | copy-start | bytes 393220
  101.1 239.2 %all-gather.24.cloned.1.call-start = ((), (), s32[]{:S(2)}) async-start(), calls=%async_computation.11 | async-start | bytes 1769472 | tf_op jit(solution)/shard_map/all_gather | solution.py:181
  144.2 29.3 %copy-start.2 = (bf16[1,128,768]{2,1,0:T(8,128)(2,1)S(1)}, bf16[1,128,768]{2,1,0:T(8,128)(2,1)}, u32[]{:S(2)}) copy-start(bf16[1,128,768]{2,1,0:T(8,128)(2,1)} %param.9) | copy-start | bytes 589828
  175.2 109.2 %copy-start.14 = (bf16[1,128,768]{2,1,0:T(8,128)(2,1)S(1)}, bf16[1,128,768]{2,1,0:T(8,128)(2,1)}, u32[]{:S(2)}) copy-start(bf16[1,128,768]{2,1,0:T(8,128)(2,1)} %param.17) | copy-start | bytes 589828
  292.3 79.2 %reduce-scatter.7.cloned.1.call-start = ((), (), s32[]{:S(2)}) async-start(), calls=%async_computation.13 | async-start | bytes 1474560 | tf_op jit(solution)/shard_map/reduce_scatter | solution.py:223
  294.9 115.8 %reduce-scatter.11.cloned.1.call-start = ((), (), s32[]{:S(2)}) async-start(), calls=%async_computation.15 | async-start | bytes 2211840 | tf_op jit(solution)/shard_map/reduce_scatter | solution.py:229
  296.9 181.7 %reduce-scatter.9.cloned.1.call-start = ((), (), s32[]{:S(2)}) async-start(), calls=%async_computation.14 | async-start | bytes 4423680 | tf_op jit(solution)/shard_map/reduce_scatter | solution.py:226
  300.9 34.1 %copy-start.5 = (f32[128,768]{0,1:T(8,128)S(1)}, f32[128,768]{0,1:T(8,128)}, u32[]{:S(2)}) copy-start(f32[128,768]{0,1:T(8,128)} %copy-done.4) | copy-start | bytes 1179652
  300.9 34.1 %copy-start.7 = (f32[128,12,64]{0,2,1:T(8,128)S(1)}, f32[128,12,64]{0,2,1:T(8,128)}, u32[]{:S(2)}) copy-start(f32[128,12,64]{0,2,1:T(8,128)} %copy-done.6) | copy-start | bytes 1179652
  300.9 246.6 %reduce-scatter.5.cloned.1.call-start = ((), (), s32[]{:S(2)}) async-start(), calls=%async_computation.12 | async-start | bytes 4423680 | tf_op jit(solution)/shard_map/reduce_scatter | solution.py:220
  370.3 177.3 %copy-start.11 = (bf16[128,1152]{1,0:T(8,128)(2,1)S(1)}, bf16[128,1152]{1,0:T(8,128)(2,1)}, u32[]{:S(2)}) copy-start(bf16[128,1152]{1,0:T(8,128)(2,1)} %get-tuple-element.27) | copy-start | bytes 884740
  370.3 177.3 %copy-start.13 = (bf16[1152,768]{1,0:T(8,128)(2,1)S(1)}, bf16[1152,768]{1,0:T(8,128)(2,1)}, u32[]{:S(2)}) copy-start(bf16[1152,768]{1,0:T(8,128)(2,1)} %all-gather.20.cloned.1.call-done) | copy-start | bytes 5308420
  370.3 246.5 %all-reduce.10.cloned.1.call-start = ((), (), s32[]{:S(2)}) async-start(), calls=%async_computation.16 | async-start | bytes 5013504 | tf_op jit(solution)/shard_map/psum | solution.py:240
  (40 other events, 256.7 us)
Sparse Core Ops, SparseCore 0:
  9.6 72.7 all-gather.9
  89.7 24.2 all-gather.13
  115.9 25.6 all-gather.11
  143.0 30.4 all-gather.15
  174.9 69.0 all-gather.17
  245.5 38.8 all-gather.19
  286.9 24.5 all-gather.21
  313.4 25.8 all-gather.23
  341.6 29.1 reduce-scatter.6
  373.6 37.0 reduce-scatter.10
  413.1 65.4 reduce-scatter.8
  480.9 66.6 reduce-scatter.4
  551.7 65.0 all-reduce.9
where the time goes:
time: 631 us; the launch traced here: 630 us
  waiting for transfers between devices  441 us (70%)
  blocking collectives  64.3 us (10%)
  matrix products  62.8 us (10%)
  other arithmetic  24.1 us (4%)
  local copies, waits for them, and re-layouts  21.3 us (3%)
  between operations  16 us (3%)
    reduce_scatter x1, waiting for transfers between devices, local(): lax.psum_scatter(local_grads[0].astype(jnp.bfloat16), 'dp', scatter_dimen...  69 us
    all_gather x1, waiting for transfers between devices, local(): lax.all_gather(shards[2], 'dp', axis=0, tiled=True)  68.1 us
    reduce_scatter x1, waiting for transfers between devices, local(): lax.psum_scatter(local_grads[2].astype(jnp.bfloat16), 'dp', scatter_dimen...  67.9 us
    all_gather x1, waiting for transfers between devices, local(): lax.all_gather(shards[0], 'dp', axis=0, tiled=True)  53.9 us
    reduce_scatter x1, waiting for transfers between devices, local(): lax.psum_scatter(local_grads[3].astype(jnp.bfloat16), 'dp', scatter_dimen...  39.2 us
    psum x1, waiting for transfers between devices, local(): lax.psum(shares[0].astype(jnp.bfloat16), 'ctx').astype(jnp.float32)  39.2 us
    all_gather x1, waiting for transfers between devices, local(): lax.all_gather(shards[3], 'dp', axis=0, tiled=True)  37.7 us
    unnamed x2, blocking collectives  24.3 us
  transfers between devices with their start and end apart: 13, of which 11 were waited for; matrix products, arithmetic and copies ran while one was open for 14% of the time, Pallas kernels for 0%

commit v1 on v0

v1 whole, which is shorter than its diff:
```python
import jax
import jax.numpy as jnp
from jax import lax
from jax.sharding import PartitionSpec as P

HEADS = 12
EPSILON = 1e-05
ROPE_THETA = 160000.0
NEGATIVE = -1e30
F32 = jnp.float32
BF = jnp.bfloat16


def dot(a, b):
    return jnp.dot(a, b, preferred_element_type=F32)


def dot_t(a, b):
    return lax.dot_general(a, b, (((1,), (1,)), ((), ())), preferred_element_type=F32)


def t_dot(a, b):
    return lax.dot_general(a, b, (((0,), (0,)), ((), ())), preferred_element_type=F32)


def normalise(values):
    average = jnp.mean(values, axis=-1, keepdims=True)
    centred = values - average
    spread = jnp.mean(centred * centred, axis=-1, keepdims=True)
    inverse = lax.rsqrt(spread + EPSILON)
    return centred * inverse, inverse


def normalise_back(unit, inverse, grad):
    mean_grad = jnp.mean(grad, axis=-1, keepdims=True)
    mean_both = jnp.mean(grad * unit, axis=-1, keepdims=True)
    return inverse * (grad - mean_grad - unit * mean_both)


def rope_tables(row_count, head_size, heads):
    position = jnp.arange(row_count, dtype=jnp.int32).astype(F32)
    frequency = ROPE_THETA ** (-jnp.arange(0, head_size, 2, dtype=F32) / head_size)
    angles = position[:, None] * frequency[None, :]
    angles = jnp.concatenate([angles, angles], axis=-1)
    return jnp.cos(angles), jnp.sin(angles)


def rotary(values, cosines, sines):
    half = values.shape[-1] // 2
    turned = jnp.concatenate([-values[..., half:], values[..., :half]], axis=-1)
    return values * cosines + turned * sines


def rotary_back(grads, cosines, sines):
    half = grads.shape[-1] // 2
    shifted = grads * sines
    return grads * cosines + jnp.concatenate([shifted[..., half:], -shifted[..., :half]], axis=-1)


def geglu(gate_in, gate_up):
    return jax.nn.gelu(gate_in, approximate=False) * gate_up


def gather_ctx(block, n_ctx):
    return lax.all_gather(block, "ctx", axis=0, tiled=False)


def scatter_ctx(blocks, n_ctx):
    return lax.psum_scatter(blocks, "ctx", scatter_dimension=0, tiled=False)


def gather_dp(block):
    return lax.all_gather(block, "dp", axis=0, tiled=True)


def scatter_dp(blocks):
    return lax.psum_scatter(blocks, "dp", scatter_dimension=0, tiled=True)


def round_up(n, m):
    return -(-n // m) * m


def make_local(n_dp, n_ctx):
    def local(hidden_in, segment_ids, w_qkv, w_out, w_in, w_down, gain_attn, gain_mlp, cotangent):
        rows, width = hidden_in.shape[1], hidden_in.shape[2]
        head_size = width // HEADS
        scale = head_size ** (-0.5)
        per = -(-HEADS // n_ctx)
        owners = HEADS // per
        tokens = rows * n_ctx
        shard = w_qkv.shape[0]
        hidden_units = w_in.shape[1] // 2
        down_rows = w_down.shape[0]
        own = down_rows // n_ctx
        padded = round_up(own, 16)
        units = n_dp * padded
        cols = per * head_size
        me = lax.axis_index("ctx")
        valid = me < owners
        slot = jnp.minimum(me, owners - 1)

        qkv_mine = lax.dynamic_slice(
            w_qkv.reshape(shard, 3, width), (0, 0, slot * cols), (shard, 3, cols)
        ).reshape(shard, 3 * cols)
        gains = jnp.stack([gain_attn, gain_mlp], axis=1)
        first = gather_dp(jnp.concatenate([qkv_mine, gains], axis=1))
        qkv_full = first[:, : 3 * cols]
        attn_gain = first[:, 3 * cols].astype(F32)[None, :]
        mlp_gain = first[:, 3 * cols + 1].astype(F32)[None, :]
        in_mine = lax.dynamic_slice(
            w_in.reshape(shard, 2 * n_dp, down_rows), (0, 0, me * own), (shard, 2 * n_dp, own)
        )
        in_mine = jnp.pad(in_mine, ((0, 0), (0, 0), (0, padded - own))).reshape(shard, 2 * units)
        in_full = gather_dp(in_mine)
        down_mine = lax.dynamic_slice(w_down, (me * own, 0), (own, width))
        down_full = gather_dp(jnp.pad(down_mine, ((0, padded - own), (0, 0))))
        out_full = lax.dynamic_slice(gather_dp(w_out), (slot * cols, 0), (cols, width))

        id_row = jnp.pad(segment_ids.astype(BF), ((0, 15), (0, width - rows)))
        packed = gather_ctx(jnp.concatenate([hidden_in[0], cotangent[0], id_row], axis=0), n_ctx)
        source = packed[:, :rows].reshape(tokens, width).astype(F32)
        upstream = packed[:, rows : 2 * rows].reshape(tokens, width)
        ids = packed[:, 2 * rows, :rows].reshape(tokens).astype(jnp.int32)

        cosines, sines = rope_tables(tokens, head_size, per)
        unit_one, inverse_one = normalise(source)
        normed_one = (unit_one * attn_gain).astype(BF)
        projected = dot(normed_one, qkv_full)

        def head_of(part, h):
            start = part * cols + h * head_size
            return projected[:, start : start + head_size]

        queries = jnp.stack([rotary(head_of(0, h), cosines, sines) for h in range(per)]).astype(BF)
        keys = jnp.stack([rotary(head_of(1, h), cosines, sines) for h in range(per)]).astype(BF)
        values = jnp.stack([head_of(2, h) for h in range(per)]).astype(BF)
        chunk = min(tokens, 1024)
        pieces = tokens // chunk
        attention, log_total = [], []
        for c in range(pieces):
            part = slice(c * chunk, (c + 1) * chunk)
            scores = jnp.einsum("hqe,hke->hqk", queries[:, part], keys, preferred_element_type=F32) * scale
            allowed = (ids[part][:, None] == ids[None, :])[None]
            scores = jnp.where(allowed, scores, NEGATIVE)
            highest = jnp.max(scores, axis=-1, keepdims=True)
            weights = jnp.where(allowed, jnp.exp(scores - highest), 0.0)
            total = jnp.sum(weights, axis=-1, keepdims=True)
            summed = jnp.einsum("hqk,hke->hqe", weights.astype(BF), values, preferred_element_type=F32)
            attention.append(summed / total)
            log_total.append(highest + jnp.log(total))
        attention_all = jnp.concatenate(attention, axis=1)
        attention_all = jnp.where(valid, attention_all, 0.0)
        attended = jnp.concatenate([attention_all[h] for h in range(per)], axis=1).astype(BF)
        branch = scatter_ctx(dot(attended, out_full).astype(BF).reshape(n_ctx, rows, width), n_ctx)
        middle = hidden_in[0].astype(F32) + branch.astype(F32)
        unit_two, inverse_two = normalise(middle)
        normed_two = gather_ctx((unit_two * mlp_gain).astype(BF), n_ctx).reshape(tokens, width)
        lifted = dot(normed_two, in_full)
        gate_in, gate_up = lifted[:, :units], lifted[:, units:]
        mixed_value, pull_gate = jax.vjp(geglu, gate_in, gate_up)
        mixed_units = mixed_value.astype(BF)
        out_part = dot(mixed_units, down_full).astype(BF)
        grad_gate_in, grad_gate_up = pull_gate(dot_t(upstream, down_full))
        grad_lifted = jnp.concatenate([grad_gate_in, grad_gate_up], axis=1).astype(BF)
        grad_normed_part = dot_t(grad_lifted, in_full).astype(BF)
        both = jnp.concatenate(
            [out_part.reshape(n_ctx, rows, width), grad_normed_part.reshape(n_ctx, rows, width)], axis=1
        )
        both = scatter_ctx(both, n_ctx).astype(F32)
        grad_in = scatter_dp(t_dot(normed_two, grad_lifted).astype(BF))
        grad_down = scatter_dp(t_dot(mixed_units, upstream).astype(BF))
        result = (middle + both[:rows]).astype(BF)
        grad_normed_two = both[rows:]
        gain_part = jnp.sum(grad_normed_two * unit_two, axis=0, keepdims=True)
        grad_middle = cotangent[0].astype(F32) + normalise_back(
            unit_two, inverse_two, grad_normed_two * mlp_gain
        )
        gain_rows = jnp.pad(gain_part.astype(BF), ((0, 15), (0, 0)))
        sent = gather_ctx(jnp.concatenate([grad_middle.astype(BF), gain_rows], axis=0), n_ctx)
        grad_branch = sent[:, :rows].reshape(tokens, width)
        mlp_gain_sum = jnp.sum(sent[:, rows].astype(F32), axis=0)
        grad_attended = dot_t(grad_branch, out_full)
        grad_heads = jnp.stack(
            [grad_attended[:, h * head_size : (h + 1) * head_size] for h in range(per)]
        ).astype(BF)
        grad_out = t_dot(attended, grad_branch).astype(BF)
        grad_queries, grad_keys, grad_values = [], 0.0, 0.0
        for c in range(pieces):
            part = slice(c * chunk, (c + 1) * chunk)
            scores = jnp.einsum("hqe,hke->hqk", queries[:, part], keys, preferred_element_type=F32) * scale
            allowed = (ids[part][:, None] == ids[None, :])[None]
            probs = jnp.where(allowed, jnp.exp(scores - log_total[c]), 0.0)
            grad_part = grad_heads[:, part]
            products = jnp.sum(grad_part.astype(F32) * attention_all[:, part], axis=-1, keepdims=True)
            grad_probs = jnp.einsum("hqe,hke->hqk", grad_part, values, preferred_element_type=F32)
            grad_scores = (probs * (grad_probs - products)).astype(BF)
            grad_queries.append(
                scale * jnp.einsum("hqk,hke->hqe", grad_scores, keys, preferred_element_type=F32)
            )
            grad_keys += scale * jnp.einsum(
                "hqk,hqe->hke", grad_scores, queries[:, part], preferred_element_type=F32
            )
            grad_values += jnp.einsum(
                "hqk,hqe->hke", probs.astype(BF), grad_part, preferred_element_type=F32
            )
        grad_queries = jnp.concatenate(grad_queries, axis=1)
        grad_projected = jnp.concatenate(
            [rotary_back(grad_queries[h], cosines, sines) for h in range(per)]
            + [rotary_back(grad_keys[h], cosines, sines) for h in range(per)]
            + [grad_values[h] for h in range(per)],
            axis=1,
        )
        grad_projected = jnp.where(valid, grad_projected, 0.0).astype(BF)
        grad_normed_one = dot_t(grad_projected, qkv_full)
        attn_gain_part = jnp.sum(grad_normed_one * unit_one, axis=0)
        back = scatter_ctx(grad_normed_one.astype(BF).reshape(n_ctx, rows, width), n_ctx).astype(F32)
        grad_qkv = t_dot(normed_one, grad_projected)
        last = scatter_dp(
            jnp.concatenate([grad_qkv, attn_gain_part[:, None]], axis=1).astype(BF)
        )
        out_all = gather_ctx(grad_out, n_ctx)[:owners].reshape(width, width)
        out_share = scatter_dp(
            jnp.concatenate([out_all, mlp_gain_sum[:, None].astype(BF)], axis=1)
        )
        unit_own, inverse_own = normalise(hidden_in[0].astype(F32))
        grad_input = grad_middle + normalise_back(unit_own, inverse_own, back * attn_gain)

        last_all = gather_ctx(last, n_ctx)
        share_qkv = last_all[:owners, :, : 3 * cols].reshape(owners, shard, 3, cols)
        share_qkv = jnp.transpose(share_qkv, (1, 2, 0, 3)).reshape(shard, 3 * width).astype(F32)
        share_attn = jnp.sum(last_all[:, :, 3 * cols].astype(F32), axis=0)
        share_out = out_share[:, :width].astype(F32)
        share_mlp = out_share[:, width].astype(F32)
        in_all = gather_ctx(grad_in, n_ctx).reshape(n_ctx, shard, 2 * n_dp, padded)[..., :own]
        share_in = jnp.transpose(in_all, (1, 2, 0, 3)).reshape(shard, 2 * hidden_units).astype(F32)
        down_all = gather_ctx(grad_down, n_ctx)[:, :own]
        share_down = down_all.reshape(down_rows, width).astype(F32)
        return (
            result[None],
            grad_input[None],
            share_qkv,
            share_out,
            share_in,
            share_down,
            share_attn,
            share_mlp,
        )

    return local


def solution(mesh):
    tokens = P("dp", "ctx", None)
    weight = P("dp", None)
    in_specs = (tokens, P("dp", "ctx")) + (weight,) * 4 + (P("dp"), P("dp"), tokens)
    out_specs = (tokens, tokens) + (weight,) * 4 + (P("dp"), P("dp"))
    return jax.shard_map(
        make_local(mesh.shape["dp"], mesh.shape["ctx"]),
        mesh=mesh,
        in_specs=in_specs,
        out_specs=out_specs,
        check_vma=False,
    )
```

time: 631 us -> 493 us (0.78); the launches traced: 630 us -> 484 us
  waiting for transfers between devices: 441 us -> 296 us
  matrix products: 62.8 us -> 38.9 us
  other arithmetic: 24.1 us -> 38.7 us
  local copies, waits for them, and re-layouts: 21.3 us -> 30.3 us
    all_gather x8 -> x7, waiting for transfers between devices: 223 us -> 110 us  [the longest x6 97 us: gather_ctx(): return lax.all_gather(block, 'ctx', axis=0, tiled=False)]
    psum x1 -> x0, waiting for transfers between devices: 39.2 us -> none  [local(): lax.psum(shares[0].astype(jnp.bfloat16), 'ctx').astype(jnp.float32)]
    all_gather x3 -> x4, blocking collectives: 27.8 us -> 63.8 us  [the longest x3 53.4 us: gather_dp(): return lax.all_gather(block, 'dp', axis=0, tiled=True)]
    unnamed x2 -> x0, blocking collectives: 24.3 us -> none
    dot_general x18, matrix products: 62.8 us -> 38.9 us  [the longest x4 7.58 us: dot_t(): lax.dot_general(a, b, (((1,), (1,)), ((), ())), preferred_element_type=F32)]
    psum x1 -> x0, blocking collectives: 12.1 us -> none  [local(): lax.psum(shares[4].astype(jnp.bfloat16), 'ctx').astype(jnp.float32)]
    all_gather x4 -> x1, local copies, waits for them, and re-layouts: 9.61 us -> 1.56 us  [gather_ctx(): return lax.all_gather(block, 'ctx', axis=0, tiled=False)]
    reduce_scatter x4 -> x7, waiting for transfers between devices: 176 us -> 184 us  [the longest x3 118 us: scatter_ctx(): return lax.psum_scatter(blocks, 'ctx', scatter_dimension=0, tiled=False)]
  transfers between devices with their start and end apart: 13 -> 14, of which waited for: 11 -> 12; matrix products, arithmetic and copies ran while one was open for 14% -> 16% of each run, Pallas kernels for 0% -> 0%
where the time goes in v1:
time: 493 us; the launch traced here: 484 us
  waiting for transfers between devices  296 us (60%)
  blocking collectives  63.8 us (13%)
  matrix products  38.9 us (8%)
  other arithmetic  38.7 us (8%)
  local copies, waits for them, and re-layouts  30.3 us (6%)
  between operations  15.4 us (3%)
    reduce_scatter x3, waiting for transfers between devices, scatter_ctx(): return lax.psum_scatter(blocks, 'ctx', scatter_dimension=0, tiled=False)  118 us
    all_gather x6, waiting for transfers between devices, gather_ctx(): return lax.all_gather(block, 'ctx', axis=0, tiled=False)  97 us
    reduce_scatter x4, waiting for transfers between devices, scatter_dp(): return lax.psum_scatter(blocks, 'dp', scatter_dimension=0, tiled=True)  65.6 us
    all_gather x3, blocking collectives, gather_dp(): return lax.all_gather(block, 'dp', axis=0, tiled=True)  53.4 us
    all_gather x1, waiting for transfers between devices, gather_dp(): return lax.all_gather(block, 'dp', axis=0, tiled=True)  12.8 us
    all_gather x1, blocking collectives, gather_ctx(): return lax.all_gather(block, 'ctx', axis=0, tiled=False)  10.5 us
  transfers between devices with their start and end apart: 14, of which 12 were waited for; matrix products, arithmetic and copies ran while one was open for 16% of the time, Pallas kernels for 0%

profile of v1, /device:TPU:0, one launch (start us, length us, event | category | flops | bytes accessed | tf_op | source)
XLA Modules:
  0.0 483.9 jit_solution(10868246656749239794)
XLA Ops:
  14.5 21.3 %all_gather.54 = bf16[768,386]{1,0:T(8,128)(2,1)S(1)} all-gather(bf16[192,386]{1,0:T(8,128)(2,1)S(1)} %pad_maximum_fusion.12), channel_id=1, replica_groups=mesh['dp'=4,'ctx'=8] {'dp'}, dimensions={0}, use_global_device_ids=true | all-gather | bytes 741120 | tf_op jit(solution)/shard_map/all_gather | solution.py:73
  36.2 10.2 %all-gather.18.cloned.1.call-done = bf16[2176,768]{1,0:T(8,128)(2,1)} async-done(((bf16[272,768]{1,0:T(8,128)(2,1)}), bf16[2176,768]{1,0:T(8,128)(2,1)}) %all-gather.18.cloned.1.call-update) | async-done | bytes 3342352 | tf_op jit(solution)/shard_map/all_gather | solution.py:65
  61.9 3.7 fusion.119
  65.6 12.8 %all-gather.14.cloned.1.call-done = bf16[768,768]{1,0:T(8,128)(2,1)} async-done(((bf16[192,768]{1,0:T(8,128)(2,1)}), bf16[768,768]{1,0:T(8,128)(2,1)}) %all-gather.14.cloned.1.call-update) | async-done | bytes 1179664 | tf_op jit(solution)/shard_map/all_gather | solution.py:73
  78.4 2.7 convolution_convert_fusion.1
  81.5 38.5 %reduce-scatter.10.cloned.1.call-done = bf16[1,128,768]{2,1,0:T(8,128)(2,1)} async-done(((bf16[8,128,768]{2,1,0:T(8,128)(2,1)}), bf16[1,128,768]{2,1,0:T(8,128)(2,1)}) %reduce-scatter.10.cloned.1.call-update) | async-done | bytes 196624 | tf_op jit(solution)/shard_map/reduce_scatter | solution.py:69
  126.4 14.7 %all_gather.58 = bf16[192,768]{1,0:T(8,128)(2,1)} all-gather(bf16[48,768]{1,0:T(8,128)(2,1)S(1)} %pad.18), channel_id=1, replica_groups=mesh['dp'=4,'ctx'=8] {'dp'}, dimensions={0}, use_global_device_ids=true | all-gather | bytes 368640 | tf_op jit(solution)/shard_map/all_gather | solution.py:73
  141.1 17.4 %all_gather.57 = bf16[768,384]{1,0:T(8,128)(2,1)} all-gather(bf16[192,384]{1,0:T(8,128)(2,1)S(1)} %copy.41), channel_id=1, replica_groups=mesh['dp'=4,'ctx'=8] {'dp'}, dimensions={0}, use_global_device_ids=true | all-gather | bytes 737280 | tf_op jit(solution)/shard_map/all_gather | solution.py:73
  160.0 2.9 fusion.120
  169.4 45.6 %reduce-scatter.12.cloned.1.call-done = bf16[1,256,768]{2,1,0:T(8,128)(2,1)} async-done(((bf16[8,256,768]{2,1,0:T(8,128)(2,1)}), bf16[1,256,768]{2,1,0:T(8,128)(2,1)}) %reduce-scatter.12.cloned.1.call-update) | async-done | bytes 393232 | tf_op jit(solution)/shard_map/reduce_scatter | solution.py:69
  219.0 3.0 convolution_convert_fusion.4
  222.3 23.3 %all-gather.20.cloned.1.call-done = bf16[1152,768]{1,0:T(8,128)(2,1)} async-done(((bf16[144,768]{1,0:T(8,128)(2,1)}), bf16[1152,768]{1,0:T(8,128)(2,1)}) %all-gather.20.cloned.1.call-update) | async-done | bytes 1769488 | tf_op jit(solution)/shard_map/all_gather | solution.py:65
  249.1 5.7 %fusion.3 = bf16[2,1024,64]{1,2,0:T(8,128)(2,1)S(1)} fusion(f32[2,1024,1024]{1,2,0:T(8,128)} %copy-done.3, f32[2,1024]{1,0:T(2,128)S(1)} %log_add_fusion, pred[1024,1024]{0,1:T(8,128)(4,1)S(1)} %broadcast_compare_fusion, bf16[1,1024,64]{1,2,0:T(8,128)(2,1)S(1)} %get-tuple-element.68, bf16[1,1024,64]{1,2,0:T(8,128)(2,1)S(1)} %get-tuple-element.67), kind=kOutput, calls=%fused_computation.7 | convolution fusion | flops 276955136 | bytes 9969664 | tf_op jit(solution)/shard_map/hqk,hqe->hke/dot_general | solution.py:204
  254.9 3.2 multiply_convert_fusion
  263.4 3.9 multiply_reduce_fusion
  274.6 20.6 %reduce-scatter.22.cloned.1.call-done = bf16[192,385]{1,0:T(8,128)(2,1)} async-done(((bf16[768,385]{1,0:T(8,128)(2,1)}), bf16[192,385]{1,0:T(8,128)(2,1)}) %reduce-scatter.22.cloned.1.call-update) | async-done | bytes 147856 | tf_op jit(solution)/shard_map/reduce_scatter | solution.py:77
  296.4 25.9 %all-gather.24.cloned.1.call-done = bf16[1024,768]{1,0:T(8,128)(2,1)} async-done(((bf16[128,768]{1,0:T(8,128)(2,1)}), bf16[1024,768]{1,0:T(8,128)(2,1)}) %all-gather.24.cloned.1.call-update) | async-done | bytes 1572880 | tf_op jit(solution)/shard_map/all_gather | solution.py:65
  324.8 19.6 %reduce-scatter.20.cloned.1.call-done = bf16[48,768]{1,0:T(8,128)(2,1)} async-done(((bf16[192,768]{1,0:T(8,128)(2,1)}), bf16[48,768]{1,0:T(8,128)(2,1)}) %reduce-scatter.20.cloned.1.call-update) | async-done | bytes 73744 | tf_op jit(solution)/shard_map/reduce_scatter | solution.py:77
  344.4 10.5 %all-gather.5 = bf16[384,768]{1,0:T(8,128)(2,1)S(1)} all-gather(bf16[48,768]{1,0:T(8,128)(2,1)} %reduce-scatter.20.cloned.1.call-done), channel_id=7, replica_groups=mesh['dp'=4,'ctx'=8] {'ctx'}, dimensions={0}, use_global_device_ids=true | all-gather | bytes 663552 | tf_op jit(solution)/shard_map/all_gather | solution.py:65
  356.0 12.8 %all-gather.26.cloned.1.call-done = bf16[1536,384]{1,0:T(8,128)(2,1)} async-done(((bf16[192,384]{1,0:T(8,128)(2,1)}), bf16[1536,384]{1,0:T(8,128)(2,1)}) %all-gather.26.cloned.1.call-update) | async-done | bytes 1179664 | tf_op jit(solution)/shard_map/all_gather | solution.py:65
  374.1 3.0 copy.52
  377.0 34.3 %reduce-scatter.14.cloned.1.call-done = bf16[1,128,768]{2,1,0:T(8,128)(2,1)} async-done(((bf16[8,128,768]{2,1,0:T(8,128)(2,1)}), bf16[1,128,768]{2,1,0:T(8,128)(2,1)}) %reduce-scatter.14.cloned.1.call-update) | async-done | bytes 196624 | tf_op jit(solution)/shard_map/reduce_scatter | solution.py:69
  414.4 24.7 %all-gather.22.cloned.1.call-done = bf16[1536,385]{1,0:T(8,128)(2,1)} async-done(((bf16[192,385]{1,0:T(8,128)(2,1)}), bf16[1536,385]{1,0:T(8,128)(2,1)}) %all-gather.22.cloned.1.call-update) | async-done | bytes 1182736 | tf_op jit(solution)/shard_map/all_gather | solution.py:65
  448.2 25.4 %reduce-scatter.16.cloned.1.call-done = bf16[192,769]{1,0:T(8,128)(2,1)} async-done(((bf16[768,769]{1,0:T(8,128)(2,1)}), bf16[192,769]{1,0:T(8,128)(2,1)}) %reduce-scatter.16.cloned.1.call-update) | async-done | bytes 295312 | tf_op jit(solution)/shard_map/reduce_scatter | solution.py:77
  (217 shorter events, 82.9 us)
Async XLA Ops:
  7.2 118.9 %copy-start = (bf16[288,768]{1,0:T(8,128)(2,1)S(1)}, bf16[288,768]{1,0:T(8,128)(2,1)}, u32[]{:S(2)}) copy-start(bf16[288,768]{1,0:T(8,128)(2,1)} %param.14) | copy-start | bytes 1327108
  7.2 39.2 %all-gather.18.cloned.1.call-start = ((), (), s32[]{:S(2)}) async-start(), calls=%async_computation.15 | async-start | bytes 3760128 | tf_op jit(solution)/shard_map/all_gather | solution.py:65
  9.8 68.7 %all-gather.14.cloned.1.call-start = ((), (), s32[]{:S(2)}) async-start(), calls=%async_computation.7 | async-start | bytes 1474560 | tf_op jit(solution)/shard_map/all_gather | solution.py:73
  10.5 109.4 %reduce-scatter.10.cloned.1.call-start = ((), (), s32[]{:S(2)}) async-start(), calls=%async_computation.8 | async-start | bytes 1769472 | tf_op jit(solution)/shard_map/reduce_scatter | solution.py:69
  65.6 58.9 %copy-start.16 = (bf16[1024,64]{0,1:T(8,128)(2,1)}, bf16[1024,64]{0,1:T(8,128)(2,1)S(1)}, u32[]{:S(2)}) copy-start(bf16[1024,64]{0,1:T(8,128)(2,1)S(1)} %get-tuple-element.70) | copy-start | bytes 393220
  81.1 78.9 %all-gather.16.cloned.1.call-start = ((), (), s32[]{:S(2)}) async-start(), calls=%async_computation.9 | async-start | bytes 1769472 | tf_op jit(solution)/shard_map/all_gather | solution.py:65
  81.5 40.1 %copy-start.33 = (f32[128]{0:T(128)}, f32[128]{0:T(128)S(1)}, u32[]{:S(2)}) copy-start(f32[128]{0:T(128)S(1)} %broadcast_multiply_fusion.4) | copy-start | bytes 1540
  124.5 90.5 %reduce-scatter.12.cloned.1.call-start = ((), (), s32[]{:S(2)}) async-start(), calls=%async_computation.10 | async-start | bytes 3538944 | tf_op jit(solution)/shard_map/reduce_scatter | solution.py:69
  169.3 46.7 %copy-start.7 = (bf16[1,128,768]{2,1,0:T(8,128)(2,1)S(1)}, bf16[1,128,768]{2,1,0:T(8,128)(2,1)}, u32[]{:S(2)}) copy-start(bf16[1,128,768]{2,1,0:T(8,128)(2,1)} %reduce-scatter.10.cloned.1.call-done) | copy-start | bytes 589828
  169.3 46.7 %copy-start.32 = (f32[128]{0:T(128)S(1)}, f32[128]{0:T(128)}, u32[]{:S(2)}) copy-start(f32[128]{0:T(128)} %copy-done.31) | copy-start | bytes 1540
  169.3 46.7 %copy-start.36 = (f32[128]{0:T(128)S(1)}, f32[128]{0:T(128)}, u32[]{:S(2)}) copy-start(f32[128]{0:T(128)} %copy-done.35) | copy-start | bytes 1540
  169.4 49.6 %copy-start.13 = (bf16[8,128,768]{2,1,0:T(8,128)(2,1)S(1)}, bf16[8,128,768]{2,1,0:T(8,128)(2,1)}, u32[]{:S(2)}) copy-start(bf16[8,128,768]{2,1,0:T(8,128)(2,1)} %all-gather.16.cloned.1.call-done) | copy-start | bytes 4718596
  169.4 76.2 %all-gather.20.cloned.1.call-start = ((), (), s32[]{:S(2)}) async-start(), calls=%async_computation.16 | async-start | bytes 1990656 | tf_op jit(solution)/shard_map/all_gather | solution.py:65
  218.9 54.4 %reduce-scatter.18.cloned.1.call-start = ((), (), s32[]{:S(2)}) async-start(), calls=%async_computation.13 | async-start | bytes 737280 | tf_op jit(solution)/shard_map/reduce_scatter | solution.py:77
  222.0 73.2 %reduce-scatter.22.cloned.1.call-start = ((), (), s32[]{:S(2)}) async-start(), calls=%async_computation.20 | async-start | bytes 983040 | tf_op jit(solution)/shard_map/reduce_scatter | solution.py:77
  269.4 52.8 %all-gather.24.cloned.1.call-start = ((), (), s32[]{:S(2)}) async-start(), calls=%async_computation.18 | async-start | bytes 1769472 | tf_op jit(solution)/shard_map/all_gather | solution.py:65
  270.6 73.8 %reduce-scatter.20.cloned.1.call-start = ((), (), s32[]{:S(2)}) async-start(), calls=%async_computation.14 | async-start | bytes 368640 | tf_op jit(solution)/shard_map/reduce_scatter | solution.py:77
  273.3 95.5 %all-gather.26.cloned.1.call-start = ((), (), s32[]{:S(2)}) async-start(), calls=%async_computation.19 | async-start | bytes 1327104 | tf_op jit(solution)/shard_map/all_gather | solution.py:65
  274.0 137.3 %reduce-scatter.14.cloned.1.call-start = ((), (), s32[]{:S(2)}) async-start(), calls=%async_computation.11 | async-start | bytes 1769472 | tf_op jit(solution)/shard_map/reduce_scatter | solution.py:69
  274.6 164.5 %all-gather.22.cloned.1.call-start = ((), (), s32[]{:S(2)}) async-start(), calls=%async_computation.17 | async-start | bytes 1769472 | tf_op jit(solution)/shard_map/all_gather | solution.py:65
  295.2 178.4 %reduce-scatter.16.cloned.1.call-start = ((), (), s32[]{:S(2)}) async-start(), calls=%async_computation.12 | async-start | bytes 1720320 | tf_op jit(solution)/shard_map/reduce_scatter | solution.py:77
  374.1 37.2 %copy-start.34 = (f32[128]{0:T(128)S(1)}, f32[128]{0:T(128)}, u32[]{:S(2)}) copy-start(f32[128]{0:T(128)} %copy-done.33) | copy-start | bytes 1540
  374.1 38.4 %copy-start.14 = (f32[128,768]{1,0:T(8,128)S(1)}, f32[128,768]{1,0:T(8,128)}, u32[]{:S(2)}) copy-start(f32[128,768]{1,0:T(8,128)} %get-tuple-element.34) | copy-start | bytes 1179652
  443.5 33.3 %copy-start.1 = (bf16[288,768]{1,0:T(8,128)(2,1)S(1)}, bf16[288,768]{1,0:T(8,128)(2,1)}, u32[]{:S(2)}) copy-start(bf16[288,768]{1,0:T(8,128)(2,1)} %param.14) | copy-start | bytes 1327108
  (33 other events, 128.9 us)
Sparse Core Ops, SparseCore 0:
  10.5 35.8 all-gather.17
  48.0 30.4 all-gather.13
  82.3 37.6 reduce-scatter.9
  124.6 25.6 all-gather.15
  169.5 45.4 reduce-scatter.11
  219.1 26.4 all-gather.19
  248.5 21.9 reduce-scatter.17
  273.5 21.6 reduce-scatter.21
  297.3 24.9 all-gather.23
  324.5 19.8 reduce-scatter.19
  346.5 22.2 all-gather.25
  372.8 38.4 reduce-scatter.13
  413.4 25.6 all-gather.21
  441.3 32.2 reduce-scatter.15

commit v2 on v1

--- a/solution.py
+++ b/solution.py
@@ -1,6 +1,10 @@
+import math
+
 import jax
 import jax.numpy as jnp
 from jax import lax
+from jax.experimental import pallas as pl
+from jax.experimental.pallas import tpu as pltpu
 from jax.sharding import PartitionSpec as P
 
 HEADS = 12
@@ -61,20 +65,271 @@
     return jax.nn.gelu(gate_in, approximate=False) * gate_up
 
 
-def gather_ctx(block, n_ctx):
-    return lax.all_gather(block, "ctx", axis=0, tiled=False)
-
-
-def scatter_ctx(blocks, n_ctx):
-    return lax.psum_scatter(blocks, "ctx", scatter_dimension=0, tiled=False)
-
-
-def gather_dp(block):
-    return lax.all_gather(block, "dp", axis=0, tiled=True)
-
-
-def scatter_dp(blocks):
-    return lax.psum_scatter(blocks, "dp", scatter_dimension=0, tiled=True)
+MESH = pl.DeviceIdType.MESH
+
+
+class Places:
+    def __init__(self, n_dp, n_ctx, send_sem, recv_sem):
+        self.n_dp, self.n_ctx, self.chips = n_dp, n_ctx, n_ctx // 2
+        self.z = lax.axis_index("dp")
+        self.me = lax.axis_index("ctx")
+        self.chip, self.core = self.me // 2, self.me % 2
+        self.sibling = self.chip * 2 + 1 - self.core
+        self.send_sem, self.recv_sem, self.used = send_sem, recv_sem, 0
+
+    def other_chip(self, d):
+        return jnp.bitwise_xor(self.chip, d)
+
+    def other_dp(self, d):
+        return jnp.bitwise_xor(self.z, d)
+
+    def copy(self, src, dst, z, ctx):
+        k = self.used
+        self.used += 1
+        return pltpu.make_async_remote_copy(
+            src_ref=src,
+            dst_ref=dst,
+            send_sem=self.send_sem.at[k],
+            recv_sem=self.recv_sem.at[k],
+            device_id=(z, ctx),
+            device_id_type=MESH,
+        )
+
+
+def run_gather_ctx(p, src, out):
+    first, second = [], []
+    for d in range(1, p.chips):
+        peer = p.other_chip(d) * 2 + p.core
+        first.append(p.copy(src, out.at[p.me], p.z, peer))
+        first[-1].start()
+    near = p.copy(src, out.at[p.me], p.z, p.sibling)
+    near.start()
+    out[p.me] = src[...]
+    yield
+    for d in range(1, p.chips):
+        first[d - 1].wait_recv()
+        held = out.at[p.other_chip(d) * 2 + p.core]
+        second.append(p.copy(held, held, p.z, p.sibling))
+        second[-1].start()
+        yield
+    for item in first:
+        item.wait_send()
+    near.wait()
+    for item in second:
+        item.wait()
+
+
+def run_scatter_ctx(p, src, out, sib, acc, land):
+    near, far = [], []
+    for d in list(range(1, p.chips)) + [0]:
+        chip = p.other_chip(d)
+        near.append(p.copy(src.at[chip * 2 + 1 - p.core], sib.at[d], p.z, p.sibling))
+        near[-1].start()
+    yield
+    for d in range(1, p.chips):
+        near[d - 1].wait_recv()
+        chip = p.other_chip(d)
+        acc[d] = (src[chip * 2 + p.core].astype(F32) + sib[d].astype(F32)).astype(acc.dtype)
+        far.append(p.copy(acc.at[d], land.at[d], p.z, chip * 2 + p.core))
+        far[-1].start()
+    near[-1].wait_recv()
+    out[...] = src[p.me].astype(F32) + sib[0].astype(F32)
+    yield
+    for d in range(1, p.chips):
+        far[d - 1].wait_recv()
+        out[...] += land[d].astype(F32)
+    for item in far + near:
+        item.wait_send()
+
+
+def run_gather_dp(p, src, out):
+    copies = []
+    for d in range(1, p.n_dp):
+        copies.append(p.copy(src, out.at[p.z], p.other_dp(d), p.me))
+        copies[-1].start()
+    out[p.z] = src[...]
+    yield
+    for item in copies:
+        item.wait()
+
+
+def run_scatter_dp(p, src, out, land):
+    copies = []
+    for d in range(1, p.n_dp):
+        copies.append(p.copy(src.at[p.other_dp(d)], land.at[d], p.other_dp(d), p.me))
+        copies[-1].start()
+    yield
+    total = src[p.z].astype(F32)
+    for d in range(1, p.n_dp):
+        copies[d - 1].wait_recv()
+        total = total + land[d].astype(F32)
+    out[...] = total.astype(out.dtype)
+    for item in copies:
+        item.wait_send()
+
+
+def run_reduce(p, src, out, land, mid):
+    yield from run_scatter_dp(p, src, mid, land)
+    yield from run_gather_ctx(p, mid, out)
+
+
+def head_place(p, s, per):
+    owners = HEADS // per
+    head = jnp.minimum(p.me, owners - 1) * per + s
+    each = HEADS // p.n_dp
+    return head // each, head % each
+
+
+def run_rows_gather(p, src, out, per):
+    size = out.shape[0] // per
+    jobs = []
+    for s in range(per):
+        owner, place = head_place(p, s, per)
+        rows = src.at[pl.ds(pl.multiple_of(place * size, size), size)]
+        slot = out.at[pl.ds(s * size, size)]
+        copies = [p.copy(rows, slot, p.other_dp(d), p.me) for d in range(1, p.n_dp)]
+        jobs.append((owner, copies))
+
+        @pl.when(p.z == owner)
+        def _():
+            for item in copies:
+                item.start()
+            out[pl.ds(s * size, size)] = src[pl.ds(pl.multiple_of(place * size, size), size)]
+
+    yield
+    for owner, copies in jobs:
+        for d in range(1, p.n_dp):
+            item = copies[d - 1]
+
+            @pl.when(p.z == owner)
+            def _():
+                item.wait_send()
+
+            @pl.when(p.other_dp(d) == owner)
+            def _():
+                item.wait_recv()
+
+
+def run_rows_scatter(p, src, out, land, per):
+    size = src.shape[0] // per
+    jobs = []
+    for s in range(per):
+        owner, _ = head_place(p, s, per)
+        slot = pl.ds(s * size, size)
+        copies = [
+            p.copy(src.at[slot], land.at[d, slot], p.other_dp(d), p.me) for d in range(1, p.n_dp)
+        ]
+        jobs.append((owner, slot, copies))
+        for d in range(1, p.n_dp):
+            item = copies[d - 1]
+
+            @pl.when(p.other_dp(d) == owner)
+            def _():
+                item.start()
+
+    yield
+    for owner, slot, copies in jobs:
+
+        @pl.when(p.z == owner)
+        def _():
+            total = src[slot].astype(F32)
+            for d in range(1, p.n_dp):
+                copies[d - 1].wait_recv()
+                total = total + land[d, slot].astype(F32)
+            out[slot] = total.astype(out.dtype)
+
+        @pl.when(p.z != owner)
+        def _():
+            out[slot] = src[slot]
+
+        for d in range(1, p.n_dp):
+            item = copies[d - 1]
+
+            @pl.when(p.other_dp(d) == owner)
+            def _():
+                item.wait_send()
+
+
+def exchange(tasks, n_dp, n_ctx, collective):
+    chips = n_ctx // 2
+    per = -(-HEADS // n_ctx)
+    outs, scratch, counts, runs, copies = [], [], [], [], 0
+    for kind, array in tasks:
+        shape, more, kept = array.shape, [], array.dtype
+        if kind == "gather_ctx":
+            shape, run, n = (n_ctx,) + shape, run_gather_ctx, 2 * chips - 1
+        elif kind == "scatter_ctx":
+            shape, run, n, kept = shape[1:], run_scatter_ctx, 2 * chips - 1, F32
+            more = [(chips,) + shape] * 3
+        elif kind == "gather_dp":
+            shape, run, n = (n_dp,) + shape, run_gather_dp, n_dp - 1
+        elif kind == "scatter_dp":
+            shape, run, n = shape[1:], run_scatter_dp, n_dp - 1
+            more = [(n_dp,) + shape]
+        elif kind == "reduce":
+            more = [shape, shape[1:]]
+            shape, run, n = (n_ctx,) + shape[1:], run_reduce, n_dp - 1 + 2 * chips - 1
+        elif kind == "rows_gather":
+            width = shape[1]
+            shape, n = (per * (width // HEADS), width), per * (n_dp - 1)
+            run = lambda *a: run_rows_gather(*a, per)
+        elif kind == "rows_scatter":
+            more, n = [(n_dp,) + shape], per * (n_dp - 1)
+            run = lambda *a: run_rows_scatter(*a, per)
+        outs.append(jax.ShapeDtypeStruct(shape, kept))
+        scratch += [pltpu.VMEM(m, array.dtype) for m in more]
+        counts.append(len(more))
+        runs.append(run)
+        copies += n
+    kinds = [kind for kind, _ in tasks]
+    use_ctx = any(k in ("gather_ctx", "scatter_ctx", "reduce") for k in kinds)
+    use_dp = any(k not in ("gather_ctx", "scatter_ctx") for k in kinds)
+
+    def kernel(*refs):
+        n = len(tasks)
+        ins, results, rest = refs[:n], refs[n : 2 * n], list(refs[2 * n :])
+        send_sem, recv_sem = rest[-2:]
+        p = Places(n_dp, n_ctx, send_sem, recv_sem)
+        barrier = pltpu.get_barrier_semaphore()
+        partners = []
+        if use_ctx:
+            partners.append((p.z, p.sibling))
+            partners += [(p.z, p.other_chip(d) * 2 + p.core) for d in range(1, chips)]
+        if use_dp:
+            partners += [(p.other_dp(d), p.me) for d in range(1, n_dp)]
+        for partner in partners:
+            pl.semaphore_signal(barrier, inc=1, device_id=partner, device_id_type=MESH)
+        pl.semaphore_wait(barrier, len(partners))
+        live = []
+        for i in range(n):
+            mine, rest = rest[: counts[i]], rest[counts[i] :]
+            live.append(runs[i](p, ins[i], results[i], *mine))
+        while live:
+            for task in list(live):
+                try:
+                    next(task)
+                except StopIteration:
+                    live.remove(task)
+
+    size = lambda shape: 2 * (math.prod(shape[:-1]) + 16) * round_up(shape[-1], 128)
+    need = sum(size(a.shape) for _, a in tasks) + sum(2 * size(o.shape) for o in outs)
+    need += sum(size(m.shape) for m in scratch)
+    sent = sum(size(a.shape) for _, a in tasks)
+    vmem = pl.BlockSpec(memory_space=pltpu.VMEM)
+    return pl.pallas_call(
+        kernel,
+        out_shape=outs,
+        in_specs=[vmem] * len(tasks),
+        out_specs=[vmem] * len(tasks),
+        scratch_shapes=scratch
+        + [pltpu.SemaphoreType.DMA((copies,)), pltpu.SemaphoreType.DMA((copies,))],
+        compiler_params=pltpu.CompilerParams(
+            collective_id=collective,
+            has_side_effects=True,
+            vmem_limit_bytes=min(60 << 20, max(16 << 20, need + need // 4 + (4 << 20))),
+        ),
+        cost_estimate=pl.CostEstimate(flops=0, bytes_accessed=4 * sent, transcendentals=0),
+    )(*[a for _, a in tasks])
 
 
 def round_up(n, m):
@@ -103,25 +358,32 @@
         qkv_mine = lax.dynamic_slice(
             w_qkv.reshape(shard, 3, width), (0, 0, slot * cols), (shard, 3, cols)
         ).reshape(shard, 3 * cols)
-        gains = jnp.stack([gain_attn, gain_mlp], axis=1)
-        first = gather_dp(jnp.concatenate([qkv_mine, gains], axis=1))
-        qkv_full = first[:, : 3 * cols]
-        attn_gain = first[:, 3 * cols].astype(F32)[None, :]
-        mlp_gain = first[:, 3 * cols + 1].astype(F32)[None, :]
+        gains = jnp.pad(jnp.stack([gain_attn, gain_mlp]), ((0, 14), (0, 0)))
         in_mine = lax.dynamic_slice(
             w_in.reshape(shard, 2 * n_dp, down_rows), (0, 0, me * own), (shard, 2 * n_dp, own)
         )
         in_mine = jnp.pad(in_mine, ((0, 0), (0, 0), (0, padded - own))).reshape(shard, 2 * units)
-        in_full = gather_dp(in_mine)
-        down_mine = lax.dynamic_slice(w_down, (me * own, 0), (own, width))
-        down_full = gather_dp(jnp.pad(down_mine, ((0, padded - own), (0, 0))))
-        out_full = lax.dynamic_slice(gather_dp(w_out), (slot * cols, 0), (cols, width))
-
-        id_row = jnp.pad(segment_ids.astype(BF), ((0, 15), (0, width - rows)))
-        packed = gather_ctx(jnp.concatenate([hidden_in[0], cotangent[0], id_row], axis=0), n_ctx)
-        source = packed[:, :rows].reshape(tokens, width).astype(F32)
-        upstream = packed[:, rows : 2 * rows].reshape(tokens, width)
-        ids = packed[:, 2 * rows, :rows].reshape(tokens).astype(jnp.int32)
+        down_mine = jnp.pad(
+            lax.dynamic_slice(w_down, (me * own, 0), (own, width)), ((0, padded - own), (0, 0))
+        )
+        id_row = jnp.pad(segment_ids.astype(BF), ((0, 15), (0, 0)))
+        hidden_all, qkv_full, gains_all, id_all, out_full, upstream = exchange(
+            [
+                ("gather_ctx", hidden_in[0]),
+                ("gather_dp", qkv_mine),
+                ("gather_dp", gains),
+                ("gather_ctx", id_row),
+                ("rows_gather", w_out),
+                ("gather_ctx", cotangent[0]),
+            ],
+            n_dp, n_ctx, 0,
+        )
+        qkv_full = qkv_full.reshape(width, 3 * cols)
+        attn_gain = gains_all[:, 0].reshape(1, width).astype(F32)
+        mlp_gain = gains_all[:, 1].reshape(1, width).astype(F32)
+        source = hidden_all.reshape(tokens, width).astype(F32)
+        upstream = upstream.reshape(tokens, width)
+        ids = id_all[:, 0].reshape(tokens).astype(jnp.int32)
 
         cosines, sines = rope_tables(tokens, head_size, per)
         unit_one, inverse_one = normalise(source)
@@ -152,10 +414,22 @@
         attention_all = jnp.concatenate(attention, axis=1)
         attention_all = jnp.where(valid, attention_all, 0.0)
         attended = jnp.concatenate([attention_all[h] for h in range(per)], axis=1).astype(BF)
-        branch = scatter_ctx(dot(attended, out_full).astype(BF).reshape(n_ctx, rows, width), n_ctx)
-        middle = hidden_in[0].astype(F32) + branch.astype(F32)
+        branch, in_full = exchange(
+            [
+                ("scatter_ctx", dot(attended, out_full).astype(BF).reshape(n_ctx, rows, width)),
+                ("gather_dp", in_mine),
+            ],
+            n_dp, n_ctx, 1,
+        )
+        in_full = in_full.reshape(width, 2 * units)
+        middle = hidden_in[0].astype(F32) + branch
         unit_two, inverse_two = normalise(middle)
-        normed_two = gather_ctx((unit_two * mlp_gain).astype(BF), n_ctx).reshape(tokens, width)
+        normed_two, down_full = exchange(
+            [("gather_ctx", (unit_two * mlp_gain).astype(BF)), ("gather_dp", down_mine)],
+            n_dp, n_ctx, 2,
+        )
+        normed_two = normed_two.reshape(tokens, width)
+        down_full = down_full.reshape(units, width)
         lifted = dot(normed_two, in_full)
         gate_in, gate_up = lifted[:, :units], lifted[:, units:]
         mixed_value, pull_gate = jax.vjp(geglu, gate_in, gate_up)
@@ -164,22 +438,31 @@
         grad_gate_in, grad_gate_up = pull_gate(dot_t(upstream, down_full))
         grad_lifted = jnp.concatenate([grad_gate_in, grad_gate_up], axis=1).astype(BF)
         grad_normed_part = dot_t(grad_lifted, in_full).astype(BF)
-        both = jnp.concatenate(
-            [out_part.reshape(n_ctx, rows, width), grad_normed_part.reshape(n_ctx, rows, width)], axis=1
-        )
-        both = scatter_ctx(both, n_ctx).astype(F32)
-        grad_in = scatter_dp(t_dot(normed_two, grad_lifted).astype(BF))
-        grad_down = scatter_dp(t_dot(mixed_units, upstream).astype(BF))
-        result = (middle + both[:rows]).astype(BF)
-        grad_normed_two = both[rows:]
+        out_sum, grad_normed_two = exchange(
+            [
+                ("scatter_ctx", grad_normed_part.reshape(n_ctx, rows, width)),
+                ("scatter_ctx", out_part.reshape(n_ctx, rows, width)),
+            ][::-1],
+            n_dp, n_ctx, 3,
+        )
+        grad_in = t_dot(normed_two, grad_lifted).astype(BF).reshape(n_dp, shard, 2 * units)
+        grad_down = t_dot(mixed_units, upstream).astype(BF).reshape(n_dp, padded, width)
+        result = (middle + out_sum).astype(BF)
         gain_part = jnp.sum(grad_normed_two * unit_two, axis=0, keepdims=True)
         grad_middle = cotangent[0].astype(F32) + normalise_back(
             unit_two, inverse_two, grad_normed_two * mlp_gain
         )
         gain_rows = jnp.pad(gain_part.astype(BF), ((0, 15), (0, 0)))
-        sent = gather_ctx(jnp.concatenate([grad_middle.astype(BF), gain_rows], axis=0), n_ctx)
-        grad_branch = sent[:, :rows].reshape(tokens, width)
-        mlp_gain_sum = jnp.sum(sent[:, rows].astype(F32), axis=0)
+        grad_branch, gain_rows, grad_in = exchange(
+            [
+                ("gather_ctx", grad_middle.astype(BF)),
+                ("gather_ctx", gain_rows),
+                ("scatter_dp", grad_in),
+            ],
+            n_dp, n_ctx, 4,
+        )
+        grad_branch = grad_branch.reshape(tokens, width)
+        mlp_gain_sum = jnp.sum(gain_rows[:, 0].astype(F32), axis=0)
         grad_attended = dot_t(grad_branch, out_full)
         grad_heads = jnp.stack(
             [grad_attended[:, h * head_size : (h + 1) * head_size] for h in range(per)]
@@ -214,28 +497,41 @@
         grad_projected = jnp.where(valid, grad_projected, 0.0).astype(BF)
         grad_normed_one = dot_t(grad_projected, qkv_full)
         attn_gain_part = jnp.sum(grad_normed_one * unit_one, axis=0)
-        back = scatter_ctx(grad_normed_one.astype(BF).reshape(n_ctx, rows, width), n_ctx).astype(F32)
-        grad_qkv = t_dot(normed_one, grad_projected)
-        last = scatter_dp(
-            jnp.concatenate([grad_qkv, attn_gain_part[:, None]], axis=1).astype(BF)
-        )
-        out_all = gather_ctx(grad_out, n_ctx)[:owners].reshape(width, width)
-        out_share = scatter_dp(
-            jnp.concatenate([out_all, mlp_gain_sum[:, None].astype(BF)], axis=1)
+        back, grad_down, grad_out, in_all = exchange(
+            [
+                ("scatter_ctx", grad_normed_one.astype(BF).reshape(n_ctx, rows, width)),
+                ("scatter_dp", grad_down),
+                ("rows_scatter", grad_out),
+                ("gather_ctx", grad_in),
+            ],
+            n_dp, n_ctx, 5,
+        )
+        grad_qkv = t_dot(normed_one, grad_projected).astype(BF).reshape(n_dp, shard, 3 * cols)
+        gain_sums = jnp.stack([attn_gain_part, mlp_gain_sum]).astype(BF).reshape(2, n_dp, shard)
+        gain_sums = jnp.pad(jnp.transpose(gain_sums, (1, 0, 2)), ((0, 0), (0, 14), (0, 0)))
+        last_all, gains_last, out_all, down_all = exchange(
+            [
+                ("reduce", grad_qkv),
+                ("reduce", gain_sums),
+                ("gather_ctx", grad_out),
+                ("gather_ctx", grad_down),
+            ],
+            n_dp, n_ctx, 6,
         )
         unit_own, inverse_own = normalise(hidden_in[0].astype(F32))
         grad_input = grad_middle + normalise_back(unit_own, inverse_own, back * attn_gain)
 
-        last_all = gather_ctx(last, n_ctx)
-        share_qkv = last_all[:owners, :, : 3 * cols].reshape(owners, shard, 3, cols)
+        share_qkv = last_all[:owners].reshape(owners, shard, 3, cols)
         share_qkv = jnp.transpose(share_qkv, (1, 2, 0, 3)).reshape(shard, 3 * width).astype(F32)
-        share_attn = jnp.sum(last_all[:, :, 3 * cols].astype(F32), axis=0)
-        share_out = out_share[:, :width].astype(F32)
-        share_mlp = out_share[:, width].astype(F32)
-        in_all = gather_ctx(grad_in, n_ctx).reshape(n_ctx, shard, 2 * n_dp, padded)[..., :own]
+        share_attn = jnp.sum(gains_last[:, 0].astype(F32), axis=0)
+        share_mlp = gains_last[0, 1].astype(F32)
+        out_rows = width // n_dp
+        share_out = lax.dynamic_slice(
+            out_all.reshape(n_ctx * cols, width), (lax.axis_index("dp") * out_rows, 0), (out_rows, width)
+        ).astype(F32)
+        in_all = in_all.reshape(n_ctx, shard, 2 * n_dp, padded)[..., :own]
         share_in = jnp.transpose(in_all, (1, 2, 0, 3)).reshape(shard, 2 * hidden_units).astype(F32)
-        down_all = gather_ctx(grad_down, n_ctx)[:, :own]
-        share_down = down_all.reshape(down_rows, width).astype(F32)
+        share_down = down_all[:, :own].reshape(down_rows, width).astype(F32)
         return (
             result[None],
             grad_input[None],

time: 493 us -> 237 us (0.48); the launches traced: 484 us -> 236 us
  waiting for transfers between devices: 296 us -> 0 us
  Pallas kernels: 0 us -> 149 us
  blocking collectives: 63.8 us -> 0 us
  other arithmetic: 38.7 us -> 23.4 us
  between operations: 15.4 us -> 1.57 us
  matrix products: 38.9 us -> 30.3 us
    reduce_scatter x7 -> x0, waiting for transfers between devices: 184 us -> none  [the longest x3 118 us: scatter_ctx(): return lax.psum_scatter(blocks, 'ctx', scatter_dimension=0, tiled=False)]
    pallas_call x0 -> x7, Pallas kernels: none -> 149 us  [exchange(): pl.pallas_call(kernel, out_shape=outs, in_specs=[vmem] * len(tasks), out_...]
    all_gather x7 -> x0, waiting for transfers between devices: 110 us -> none  [the longest x6 97 us: gather_ctx(): return lax.all_gather(block, 'ctx', axis=0, tiled=False)]
    all_gather x4 -> x0, blocking collectives: 63.8 us -> none  [the longest x3 53.4 us: gather_dp(): return lax.all_gather(block, 'dp', axis=0, tiled=True)]
    slice x6 -> x0, local copies, waits for them, and re-layouts: 6.63 us -> none  [the longest x1 1.57 us: local(): grad_branch = sent[:, :rows].reshape(tokens, width)]
    concatenate x6 -> x0, other arithmetic: 5.78 us -> none  [the longest x1 1.9 us: local(): jnp.concatenate([out_part.reshape(n_ctx, rows, width), grad_normed_part.r...]
    convert_element_type x2 -> x3, local copies, waits for them, and re-layouts: 4.04 us -> 9.19 us  [local(): jnp.transpose(share_qkv, (1, 2, 0, 3)).reshape(shard, 3 * width).astype(F32)]
  transfers between devices with their start and end apart: 14 -> 0, of which waited for: 12 -> 0; matrix products, arithmetic and copies ran while one was open for 16% -> 0% of each run, Pallas kernels for 0% -> 0%
where the time goes in v2:
time: 237 us; the launch traced here: 236 us
  Pallas kernels  149 us (63%)
  local copies, waits for them, and re-layouts  32.1 us (14%)
  matrix products  30.3 us (13%)
  other arithmetic  23.4 us (10%)
    pallas_call x7, Pallas kernels, exchange(): pl.pallas_call(kernel, out_shape=outs, in_specs=[vmem] * len(tasks), out_...  149 us
    convert_element_type x3, local copies, waits for them, and re-layouts, local(): jnp.transpose(share_qkv, (1, 2, 0, 3)).reshape(shard, 3 * width).astype(F32)  9.19 us
    unnamed x83, local copies, waits for them, and re-layouts  8.29 us
    dot_general x4, matrix products, dot_t(): lax.dot_general(a, b, (((1,), (1,)), ((), ())), preferred_element_type=F32)  5.77 us
    dot_general x1, matrix products, local(): jnp.einsum('hqk,hqe->hke', probs.astype(BF), grad_part, preferred_element...  5.63 us
    dot_general x1, matrix products, local(): jnp.einsum('hqe,hke->hqk', grad_part, values, preferred_element_type=F32)  5.38 us
    convert_element_type x2, local copies, waits for them, and re-layouts, local(): jnp.transpose(in_all, (1, 2, 0, 3)).reshape(shard, 2 * hidden_units)  5.18 us

profile of v2, /device:TPU:0, one launch (start us, length us, event | category | flops | bytes accessed | tf_op | source)
XLA Modules:
  0.0 236.3 jit_solution(3406736552324526114)
XLA Ops:
  6.1 2.2 reshape.275
  12.5 27.4 %shard_map.152 = (bf16[8,128,768]{2,1,0:T(8,128)(2,1)S(1)}, bf16[4,192,384]{2,1,0:T(8,128)(2,1)S(1)}, bf16[4,16,192]{2,1,0:T(8,128)(2,1)S(1)}, bf16[8,16,128]{2,...) custom-call(bf16[128,768]{1,0:T(8,128)(2,1)S(1)} %bitcast.133, ...), custom_call_target="tpu_custom_call" | custom-call | bytes 3784704 | tf_op jit(solution)/shard_map/pallas_call | solution.py:319
  50.2 1.9 select_reduce_fusion
  52.1 2.3 fusion.1
  55.4 2.9 %fusion.102 = (bf16[2,1024,64]{1,2,0:T(8,128)(2,1)S(1)}, f32[2,1024,64]{1,2,0:T(8,128)S(1)}) fusion(f32[2,1024]{1,0:T(2,128)S(1)} %fusion.1, f32[2,1024,1024]{1,2,0:T(8,128)S(1)} %get-tuple-element.118, f32[2,1024]{1,0:T(2,128)S(1)} %get-tuple-element.117, pred[1024,1024]{0,1:T(8,128)(4,1)S(1)} %broadcast_compare_fusion, ...), kind=kOutput, calls=%fused_computation.204 | convolution fusion | flops 279838720 | bytes 10502145 | tf_op jit(solution)/shard_map/hqk,hke->hqe/dot_general | solution.py:411
  59.1 18.9 %shard_map.153 = (f32[128,768]{1,0:T(8,128)S(1)}, bf16[4,192,384]{2,1,0:T(8,128)(2,1)S(1)}) custom-call(bf16[8,128,768]{2,1,0:T(8,128)(2,1)S(1)} %bitcast.132, bf16[192,384]{1,0:T(8,128)(2,1)S(1)} %copy-done.11), custom_call_target="tpu_custom_call" | custom-call | bytes 7028736 | tf_op jit(solution)/shard_map/pallas_call | solution.py:319
  79.1 15.4 %shard_map.154 = (bf16[8,128,768]{2,1,0:T(8,128)(2,1)S(1)}, bf16[4,48,768]{2,1,0:T(8,128)(2,1)S(1)}) custom-call(bf16[128,768]{1,0:T(8,128)(2,1)S(1)} %multiply_convert_fusion.5.refs_0_, bf16[48,768]{1,0:T(8,128)(2,1)S(1)} %copy-done.13), custom_call_target="tpu_custom_call" | custom-call | bytes 1277952 | tf_op jit(solution)/shard_map/pallas_call | solution.py:319
  95.3 2.7 %add_convert_fusion = (bf16[1024,192]{0,1:T(8,128)(2,1)S(1)}, f32[1024,192]{0,1:T(8,128)S(1)}, f32[1024,192]{0,1:T(8,128)S(1)}) fusion(f32[1024,384]{0,1:T(8,128)S(1)} %fusion.103, bf16[1024,768]{1,0:T(8,128)(2,1)S(1)} %bitcast.136, bf16[192,768]{1,0:T(8,128)(2,1)S(1)} %bitcast.149), kind=kOutput, calls=%fused_computation.38 | convolution fusion | flops 316342272 | bytes 5406720 | tf_op jit(solution)/shard_map/dot_general | solution.py:23
  102.3 22.5 %shard_map.155 = (f32[128,768]{1,0:T(8,128)S(1)}, f32[128,768]{1,0:T(8,128)S(1)}) custom-call(bf16[8,128,768]{2,1,0:T(8,128)(2,1)S(1)} %bitcast.129, bf16[8,128,768]{2,1,0:T(8,128)(2,1)S(1)} %bitcast.138), custom_call_target="tpu_custom_call" | custom-call | bytes 12779520 | tf_op jit(solution)/shard_map/pallas_call | solution.py:319
  126.0 15.8 %shard_map.156 = (bf16[8,128,768]{2,1,0:T(8,128)(2,1)S(1)}, bf16[8,16,768]{2,1,0:T(8,128)(2,1)S(1)}, bf16[192,384]{1,0:T(8,128)(2,1)S(1)}) custom-call(bf16[128,768]{1,0:T(8,128)(2,1)S(1)} %get-tuple-element.69.refs_0_, bf16[16,768]{1,0:T(8,128)(2,1)S(1)} %pad.28.refs_1_, bf16[4,192,384]{2,1,0:T(8,128)(2,1)S(1)} %bitcast.147), custom_call_target="tpu_custom_call" | custom-call | bytes 3489792 | tf_op jit(solution)/shard_map/pallas_call | solution.py:319
  143.2 5.6 %fusion.3 = bf16[2,1024,64]{1,2,0:T(8,128)(2,1)S(1)} fusion(f32[2,1024,1024]{1,2,0:T(8,128)} %copy-done.16, f32[2,1024]{1,0:T(2,128)S(1)} %log_add_fusion, pred[1024,1024]{0,1:T(8,128)(4,1)S(1)} %copy-done.18, bf16[1,1024,64]{1,2,0:T(8,128)(2,1)S(1)} %get-tuple-element.107, bf16[1,1024,64]{1,2,0:T(8,128)(2,1)S(1)} %get-tuple-element.106), kind=kOutput, calls=%fused_computation.7 | convolution fusion | flops 276955136 | bytes 9969664 | tf_op jit(solution)/shard_map/hqk,hqe->hke/dot_general | solution.py:487
  148.9 5.4 %multiply_convert_fusion = bf16[2,1024,1024]{1,2,0:T(8,128)(2,1)S(1)} fusion(f32[2,1024,1024]{1,2,0:T(8,128)} %copy-done.16, f32[2,1024]{1,0:T(2,128)S(1)} %multiply_reduce_fusion.2, f32[2,1024]{1,0:T(2,128)S(1)} %log_add_fusion, pred[1024,1024]{0,1:T(8,128)(4,1)S(1)} %copy-done.18, bf16[1,1024,64]{1,2,0:T(8,128)(2,1)S(1)} %copy-done.32, ...), kind=kOutput, calls=%fused_computation | convolution fusion | flops 281280512 | bytes 14172160 | tf_op jit(solution)/shard_map/hqe,hke->hqk/dot_general | solution.py:479
  154.3 1.4 convolution_multiply_fusion.1
  159.9 1.4 multiply_reduce_fusion
  162.4 22.4 %shard_map.157 = (f32[128,768]{1,0:T(8,128)S(1)}, bf16[48,768]{1,0:T(8,128)(2,1)S(1)}, bf16[128,768]{1,0:T(8,128)(2,1)S(1)}, bf16[8,192,384]{2,1,0:T(8,128)(2,1)S(1)}) custom-call(bf16[8,128,768]{2,1,0:T(8,128)(2,1)S(1)} %bitcast.139, bf16[4,48,768]{2,1,0:T(8,128)(2,1)S(1)} %bitcast.140, bf16[128,768]{1,0:T(8,128)(2,1)S(1)} %convolution_convert_fusion.7.refs_2_, ...), custom_call_target="tpu_custom_call" | custom-call | bytes 9191424 | tf_op jit(solution)/shard_map/pallas_call | solution.py:319
  186.1 1.6 copy.34
  187.7 1.6 convert_bitcast_fusion
  189.3 1.8 copy.35
  191.1 3.4 %reshape.299 = f32[192,2304]{0,1:T(8,128)} reshape(f32[192,8,8,36]{0,3,2,1:T(8,128)} %copy.35) | data formatting | bytes 3538944 | tf_op jit(solution)/shard_map/convert_element_type | solution.py:533
  194.5 2.9 %copy.36 = f32[192,2304]{1,0:T(8,128)} copy(f32[192,2304]{0,1:T(8,128)} %reshape.299) | data formatting | bytes 3538944
  197.4 26.5 %shard_map.158 = (bf16[8,192,384]{2,1,0:T(8,128)(2,1)S(1)}, bf16[8,16,192]{2,1,0:T(8,128)(2,1)S(1)}, bf16[8,128,768]{2,1,0:T(8,128)(2,1)S(1)}, bf16[8,48,768]{2,1,0:T(8,128)(2,1)S(1)}) custom-call(bf16[4,192,384]{2,1,0:T(8,128)(2,1)S(1)} %bitcast.146, bf16[4,16,192]{2,1,0:T(8,128)(2,1)S(1)} %pad.29.refs_1_, bf16[128,768]{1,0:T(8,128)(2,1)S(1)} %get-tuple-element.47.refs_2_, ...), custom_call_target="tpu_custom_call" | custom-call | bytes 3850240 | tf_op jit(solution)/shard_map/pallas_call | solution.py:319
  226.0 2.3 reshape.302
  228.3 4.1 %copy.33 = f32[192,3,6,128]{3,2,1,0:T(8,128)} copy(f32[192,3,6,128]{3,1,0,2:T(4,128)} %bitcast.152) | data formatting | bytes 3538944 | tf_op jit(solution)/shard_map/convert_element_type | solution.py:525
  232.4 2.8 %reshape.298 = f32[192,2304]{1,0:T(8,128)} reshape(f32[192,3,6,128]{3,2,1,0:T(8,128)} %copy.33) | data formatting | bytes 3538944 | tf_op jit(solution)/shard_map/convert_element_type | solution.py:525
  (165 shorter events, 39.6 us)
Async XLA Ops:
  0.6 4.8 %copy-start = (bf16[288,768]{1,0:T(8,128)(2,1)S(1)}, bf16[288,768]{1,0:T(8,128)(2,1)}, u32[]{:S(2)}) copy-start(bf16[288,768]{1,0:T(8,128)(2,1)} %param.14) | copy-start | bytes 1327108
  0.7 8.5 %copy-start.20 = (bf16[192,2304]{1,0:T(8,128)(2,1)S(1)}, bf16[192,2304]{1,0:T(8,128)(2,1)}, u32[]{:S(2)}) copy-start(bf16[192,2304]{1,0:T(8,128)(2,1)} %param.13) | copy-start | bytes 2654212
  6.1 4.5 %copy-start.2 = (bf16[1,128,768]{2,1,0:T(8,128)(2,1)S(1)}, bf16[1,128,768]{2,1,0:T(8,128)(2,1)}, u32[]{:S(2)}) copy-start(bf16[1,128,768]{2,1,0:T(8,128)(2,1)} %param.9) | copy-start | bytes 589828
  6.1 4.5 %copy-start.4 = (bf16[1,128,768]{2,1,0:T(8,128)(2,1)S(1)}, bf16[1,128,768]{2,1,0:T(8,128)(2,1)}, u32[]{:S(2)}) copy-start(bf16[1,128,768]{2,1,0:T(8,128)(2,1)} %param.17) | copy-start | bytes 589828
  45.6 8.8 %copy-start.17 = (pred[1024,1024]{0,1:T(8,128)(4,1)}, pred[1024,1024]{0,1:T(8,128)(4,1)S(1)}, u32[]{:S(2)}) copy-start(pred[1024,1024]{0,1:T(8,128)(4,1)S(1)} %broadcast_compare_fusion) | copy-start | bytes 3145732
  47.7 6.7 %copy-start.29 = (bf16[1,1024,64]{1,2,0:T(8,128)(2,1)}, bf16[1,1024,64]{1,2,0:T(8,128)(2,1)S(1)}, u32[]{:S(2)}) copy-start(bf16[1,1024,64]{1,2,0:T(8,128)(2,1)S(1)} %get-tuple-element.91) | copy-start | bytes 393220
  47.8 6.7 %copy-start.31 = (bf16[1,1024,64]{1,2,0:T(8,128)(2,1)}, bf16[1,1024,64]{1,2,0:T(8,128)(2,1)S(1)}, u32[]{:S(2)}) copy-start(bf16[1,1024,64]{1,2,0:T(8,128)(2,1)S(1)} %get-tuple-element.92) | copy-start | bytes 393220
  47.9 2.3 copy-start.14
  49.1 3.0 %copy-start.21 = (bf16[1,1024,64]{1,2,0:T(8,128)(2,1)}, bf16[1,1024,64]{1,2,0:T(8,128)(2,1)S(1)}, u32[]{:S(2)}) copy-start(bf16[1,1024,64]{1,2,0:T(8,128)(2,1)S(1)} %get-tuple-element.81) | copy-start | bytes 393220
  49.2 3.0 %copy-start.23 = (bf16[1,1024,64]{1,2,0:T(8,128)(2,1)}, bf16[1,1024,64]{1,2,0:T(8,128)(2,1)S(1)}, u32[]{:S(2)}) copy-start(bf16[1,1024,64]{1,2,0:T(8,128)(2,1)S(1)} %get-tuple-element.79) | copy-start | bytes 393220
  49.2 3.0 %copy-start.25 = (bf16[1,1024,64]{1,2,0:T(8,128)(2,1)}, bf16[1,1024,64]{1,2,0:T(8,128)(2,1)S(1)}, u32[]{:S(2)}) copy-start(bf16[1,1024,64]{1,2,0:T(8,128)(2,1)S(1)} %get-tuple-element.80) | copy-start | bytes 393220
  50.2 1.9 copy-start.27
  52.1 3.2 %copy-start.16 = (f32[2,1024,1024]{1,2,0:T(8,128)}, f32[2,1024,1024]{1,2,0:T(8,128)S(1)}, u32[]{:S(2)}) copy-start(f32[2,1024,1024]{1,2,0:T(8,128)S(1)} %get-tuple-element.118) | copy-start | bytes 25165828
  55.4 2.9 %copy-start.6 = (bf16[128,768]{1,0:T(8,128)(2,1)S(1)}, bf16[128,768]{1,0:T(8,128)(2,1)}, u32[]{:S(2)}) copy-start(bf16[128,768]{1,0:T(8,128)(2,1)} %copy-done.5) | copy-start | bytes 589828
  58.2 19.8 %copy-start.34 = (f32[128]{0:T(128)S(1)}, f32[128]{0:T(128)}, u32[]{:S(2)}) copy-start(f32[128]{0:T(128)} %broadcast_multiply_fusion.4) | copy-start | bytes 1540
  58.3 20.8 %copy-start.13 = (bf16[48,768]{1,0:T(8,128)(2,1)S(1)}, bf16[48,768]{1,0:T(8,128)(2,1)}, u32[]{:S(2)}) copy-start(bf16[48,768]{1,0:T(8,128)(2,1)} %pad.27.refs_1_) | copy-start | bytes 221188
  143.2 5.6 %copy-start.30 = (bf16[1,1024,64]{1,2,0:T(8,128)(2,1)S(1)}, bf16[1,1024,64]{1,2,0:T(8,128)(2,1)}, u32[]{:S(2)}) copy-start(bf16[1,1024,64]{1,2,0:T(8,128)(2,1)} %copy-done.29) | copy-start | bytes 393220
  143.2 5.6 %copy-start.32 = (bf16[1,1024,64]{1,2,0:T(8,128)(2,1)S(1)}, bf16[1,1024,64]{1,2,0:T(8,128)(2,1)}, u32[]{:S(2)}) copy-start(bf16[1,1024,64]{1,2,0:T(8,128)(2,1)} %copy-done.31) | copy-start | bytes 393220
  148.9 5.4 %copy-start.24 = (bf16[1,1024,64]{1,2,0:T(8,128)(2,1)S(1)}, bf16[1,1024,64]{1,2,0:T(8,128)(2,1)}, u32[]{:S(2)}) copy-start(bf16[1,1024,64]{1,2,0:T(8,128)(2,1)} %copy-done.23) | copy-start | bytes 393220
  148.9 5.4 %copy-start.26 = (bf16[1,1024,64]{1,2,0:T(8,128)(2,1)S(1)}, bf16[1,1024,64]{1,2,0:T(8,128)(2,1)}, u32[]{:S(2)}) copy-start(bf16[1,1024,64]{1,2,0:T(8,128)(2,1)} %copy-done.25) | copy-start | bytes 393220
  161.4 23.5 %copy-start.35 = (f32[128]{0:T(128)S(1)}, f32[128]{0:T(128)}, u32[]{:S(2)}) copy-start(f32[128]{0:T(128)} %broadcast_multiply_fusion.4) | copy-start | bytes 1540
  161.4 23.4 %copy-start.38 = (f32[128]{0:T(128)S(1)}, f32[128]{0:T(128)}, u32[]{:S(2)}) copy-start(f32[128]{0:T(128)} %add_rsqrt_fusion.1) | copy-start | bytes 1540
  162.4 22.6 %copy-start.19 = (f32[128,768]{1,0:T(8,128)S(1)}, f32[128,768]{1,0:T(8,128)}, u32[]{:S(2)}) copy-start(f32[128,768]{1,0:T(8,128)} %get-tuple-element.70) | copy-start | bytes 1179652
  232.4 3.9 %copy-start.1 = (bf16[288,768]{1,0:T(8,128)(2,1)S(1)}, bf16[288,768]{1,0:T(8,128)(2,1)}, u32[]{:S(2)}) copy-start(bf16[288,768]{1,0:T(8,128)(2,1)} %param.14) | copy-start | bytes 1327108
  (16 other events, 18.7 us)

commit v3 on v2

--- a/solution.py
+++ b/solution.py
@@ -250,11 +250,47 @@
                 item.wait_send()
 
 
+def place_columns(parts, own):
+    def place(buf, res):
+        n, width = buf.shape[0], buf.shape[2] // parts
+        for j in range(n):
+            block = buf[j].astype(F32)
+            for p in range(parts):
+                res[:, (p * n + j) * own : (p * n + j + 1) * own] = block[:, p * width : p * width + own]
+
+    return place
+
+
+def place_rows(own):
+    def place(buf, res):
+        for j in range(buf.shape[0]):
+            res[j * own : (j + 1) * own, :] = buf[j].astype(F32)[:own]
+
+    return place
+
+
+def run_gather_place(p, src, res, buf, place):
+    yield from run_gather_ctx(p, src, buf)
+    place(buf, res)
+
+
+def run_reduce_place(p, src, res, land, mid, buf, place):
+    yield from run_scatter_dp(p, src, mid, land)
+    yield from run_gather_ctx(p, mid, buf)
+    place(buf, res)
+
+
+def run_rows_reduce(p, src, out, land, mid, per):
+    yield from run_rows_scatter(p, src, mid, land, per)
+    yield from run_gather_ctx(p, mid, out)
+
+
 def exchange(tasks, n_dp, n_ctx, collective):
     chips = n_ctx // 2
     per = -(-HEADS // n_ctx)
     outs, scratch, counts, runs, copies = [], [], [], [], 0
-    for kind, array in tasks:
+    for task in tasks:
+        kind, array = task[:2]
         shape, more, kept = array.shape, [], array.dtype
         if kind == "gather_ctx":
             shape, run, n = (n_ctx,) + shape, run_gather_ctx, 2 * chips - 1
@@ -269,21 +305,30 @@
         elif kind == "reduce":
             more = [shape, shape[1:]]
             shape, run, n = (n_ctx,) + shape[1:], run_reduce, n_dp - 1 + 2 * chips - 1
+        elif kind == "reduce_place":
+            more = [shape, shape[1:], (n_ctx,) + shape[1:]]
+            shape, n, kept = task[3], n_dp - 1 + 2 * chips - 1, F32
+            run = lambda *a, place=task[2]: run_reduce_place(*a, place)
+        elif kind == "gather_place":
+            more = [(n_ctx,) + shape]
+            shape, n, kept = task[3], 2 * chips - 1, F32
+            run = lambda *a, place=task[2]: run_gather_place(*a, place)
+        elif kind == "rows_reduce":
+            more, n = [(n_dp,) + shape, shape], per * (n_dp - 1) + 2 * chips - 1
+            shape = (n_ctx,) + shape
+            run = lambda *a: run_rows_reduce(*a, per)
         elif kind == "rows_gather":
             width = shape[1]
             shape, n = (per * (width // HEADS), width), per * (n_dp - 1)
             run = lambda *a: run_rows_gather(*a, per)
-        elif kind == "rows_scatter":
-            more, n = [(n_dp,) + shape], per * (n_dp - 1)
-            run = lambda *a: run_rows_scatter(*a, per)
         outs.append(jax.ShapeDtypeStruct(shape, kept))
         scratch += [pltpu.VMEM(m, array.dtype) for m in more]
         counts.append(len(more))
         runs.append(run)
         copies += n
-    kinds = [kind for kind, _ in tasks]
-    use_ctx = any(k in ("gather_ctx", "scatter_ctx", "reduce") for k in kinds)
-    use_dp = any(k not in ("gather_ctx", "scatter_ctx") for k in kinds)
+    kinds = [task[0] for task in tasks]
+    use_ctx = any(k not in ("gather_dp", "scatter_dp", "rows_gather") for k in kinds)
+    use_dp = any(k not in ("gather_ctx", "scatter_ctx", "gather_place") for k in kinds)
 
     def kernel(*refs):
         n = len(tasks)
@@ -312,9 +357,9 @@
                     live.remove(task)
 
     size = lambda shape: 2 * (math.prod(shape[:-1]) + 16) * round_up(shape[-1], 128)
-    need = sum(size(a.shape) for _, a in tasks) + sum(2 * size(o.shape) for o in outs)
+    need = sum(2 * size(task[1].shape) for task in tasks) + sum(2 * size(o.shape) for o in outs)
     need += sum(size(m.shape) for m in scratch)
-    sent = sum(size(a.shape) for _, a in tasks)
+    sent = sum(size(task[1].shape) for task in tasks)
     vmem = pl.BlockSpec(memory_space=pltpu.VMEM)
     return pl.pallas_call(
         kernel,
@@ -329,7 +374,7 @@
             vmem_limit_bytes=min(60 << 20, max(16 << 20, need + need // 4 + (4 << 20))),
         ),
         cost_estimate=pl.CostEstimate(flops=0, bytes_accessed=4 * sent, transcendentals=0),
-    )(*[a for _, a in tasks])
+    )(*[task[1] for task in tasks])
 
 
 def round_up(n, m):
@@ -438,26 +483,27 @@
         grad_gate_in, grad_gate_up = pull_gate(dot_t(upstream, down_full))
         grad_lifted = jnp.concatenate([grad_gate_in, grad_gate_up], axis=1).astype(BF)
         grad_normed_part = dot_t(grad_lifted, in_full).astype(BF)
-        out_sum, grad_normed_two = exchange(
+        grad_in = t_dot(normed_two, grad_lifted).astype(BF).reshape(n_dp, shard, 2 * units)
+        grad_down = t_dot(mixed_units, upstream).astype(BF).reshape(n_dp, padded, width)
+        grad_normed_two, out_sum, grad_in = exchange(
             [
                 ("scatter_ctx", grad_normed_part.reshape(n_ctx, rows, width)),
                 ("scatter_ctx", out_part.reshape(n_ctx, rows, width)),
-            ][::-1],
+                ("scatter_dp", grad_in),
+            ],
             n_dp, n_ctx, 3,
         )
-        grad_in = t_dot(normed_two, grad_lifted).astype(BF).reshape(n_dp, shard, 2 * units)
-        grad_down = t_dot(mixed_units, upstream).astype(BF).reshape(n_dp, padded, width)
         result = (middle + out_sum).astype(BF)
         gain_part = jnp.sum(grad_normed_two * unit_two, axis=0, keepdims=True)
         grad_middle = cotangent[0].astype(F32) + normalise_back(
             unit_two, inverse_two, grad_normed_two * mlp_gain
         )
         gain_rows = jnp.pad(gain_part.astype(BF), ((0, 15), (0, 0)))
-        grad_branch, gain_rows, grad_in = exchange(
+        grad_branch, gain_rows, grad_down = exchange(
             [
                 ("gather_ctx", grad_middle.astype(BF)),
                 ("gather_ctx", gain_rows),
-                ("scatter_dp", grad_in),
+                ("scatter_dp", grad_down),
             ],
             n_dp, n_ctx, 4,
         )
@@ -497,41 +543,37 @@
         grad_projected = jnp.where(valid, grad_projected, 0.0).astype(BF)
         grad_normed_one = dot_t(grad_projected, qkv_full)
         attn_gain_part = jnp.sum(grad_normed_one * unit_one, axis=0)
-        back, grad_down, grad_out, in_all = exchange(
-            [
-                ("scatter_ctx", grad_normed_one.astype(BF).reshape(n_ctx, rows, width)),
-                ("scatter_dp", grad_down),
-                ("rows_scatter", grad_out),
-                ("gather_ctx", grad_in),
-            ],
-            n_dp, n_ctx, 5,
-        )
         grad_qkv = t_dot(normed_one, grad_projected).astype(BF).reshape(n_dp, shard, 3 * cols)
         gain_sums = jnp.stack([attn_gain_part, mlp_gain_sum]).astype(BF).reshape(2, n_dp, shard)
         gain_sums = jnp.pad(jnp.transpose(gain_sums, (1, 0, 2)), ((0, 0), (0, 14), (0, 0)))
-        last_all, gains_last, out_all, down_all = exchange(
+
+        def place_heads(buf, res):
+            for j in range(owners):
+                block = buf[j].astype(F32)
+                for part in range(3):
+                    start = part * width + j * cols
+                    res[:, start : start + cols] = block[:, part * cols : (part + 1) * cols]
+
+        back, share_in, share_qkv, out_all, gains_last, share_down = exchange(
             [
-                ("reduce", grad_qkv),
+                ("scatter_ctx", grad_normed_one.astype(BF).reshape(n_ctx, rows, width)),
+                ("gather_place", grad_in, place_columns(2 * n_dp, own), (shard, 2 * hidden_units)),
+                ("reduce_place", grad_qkv, place_heads, (shard, 3 * width)),
+                ("rows_reduce", grad_out),
                 ("reduce", gain_sums),
-                ("gather_ctx", grad_out),
-                ("gather_ctx", grad_down),
+                ("gather_place", grad_down, place_rows(own), (down_rows, width)),
             ],
-            n_dp, n_ctx, 6,
+            n_dp, n_ctx, 5,
         )
         unit_own, inverse_own = normalise(hidden_in[0].astype(F32))
         grad_input = grad_middle + normalise_back(unit_own, inverse_own, back * attn_gain)
 
-        share_qkv = last_all[:owners].reshape(owners, shard, 3, cols)
-        share_qkv = jnp.transpose(share_qkv, (1, 2, 0, 3)).reshape(shard, 3 * width).astype(F32)
         share_attn = jnp.sum(gains_last[:, 0].astype(F32), axis=0)
         share_mlp = gains_last[0, 1].astype(F32)
         out_rows = width // n_dp
         share_out = lax.dynamic_slice(
             out_all.reshape(n_ctx * cols, width), (lax.axis_index("dp") * out_rows, 0), (out_rows, width)
         ).astype(F32)
-        in_all = in_all.reshape(n_ctx, shard, 2 * n_dp, padded)[..., :own]
-        share_in = jnp.transpose(in_all, (1, 2, 0, 3)).reshape(shard, 2 * hidden_units).astype(F32)
-        share_down = down_all[:, :own].reshape(down_rows, width).astype(F32)
         return (
             result[None],
             grad_input[None],

time: 237 us -> 212 us (0.89)
  local copies, waits for them, and re-layouts: 32.1 us -> 15.9 us
  Pallas kernels: 149 us -> 141 us
    convert_element_type x6 -> x0, local copies, waits for them, and re-layouts: 15.4 us -> none  [the longest x3 9.19 us: local(): jnp.transpose(share_qkv, (1, 2, 0, 3)).reshape(shard, 3 * width).astype(F32)]
    pallas_call x7 -> x6, Pallas kernels: 149 us -> 141 us  [exchange(): pl.pallas_call(kernel, out_shape=outs, in_specs=[vmem] * len(tasks), out_...]
    unnamed x83 -> x97, local copies, waits for them, and re-layouts: 8.29 us -> 9.11 us
where the time goes in v3:
time: 212 us
  Pallas kernels  141 us (67%)
  matrix products  28.8 us (14%)
  other arithmetic  24.6 us (12%)
  local copies, waits for them, and re-layouts  15.9 us (8%)
    pallas_call x6, Pallas kernels, exchange(): pl.pallas_call(kernel, out_shape=outs, in_specs=[vmem] * len(tasks), out_...  141 us
    unnamed x97, local copies, waits for them, and re-layouts  9.11 us
    dot_general x1, matrix products, local(): jnp.einsum('hqk,hqe->hke', probs.astype(BF), grad_part, preferred_element...  5.62 us
    dot_general x1, matrix products, local(): jnp.einsum('hqe,hke->hqk', grad_part, values, preferred_element_type=F32)  5.32 us

profile of v3, /device:TPU:0, one launch (start us, length us, event | category | flops | bytes accessed | tf_op | source)
XLA Modules:
  0.0 212.0 jit_solution(9108183648680657413)
XLA Ops:
  1.4 1.0 convert_reduce_fusion.1
  6.2 2.2 %reshape.260 = bf16[192,3,768]{2,1,0:T(4,128)(2,1)S(1)} reshape(bf16[192,2304]{1,0:T(8,128)(2,1)} %param.11) | data formatting | bytes 1769472 | tf_op jit(solution)/shard_map/reshape | solution.py:404
  12.5 27.4 %shard_map.152 = (bf16[8,128,768]{2,1,0:T(8,128)(2,1)S(1)}, bf16[4,192,384]{2,1,0:T(8,128)(2,1)S(1)}, bf16[4,16,192]{2,1,0:T(8,128)(2,1)S(1)}, bf16[8,16,128]{2,...) custom-call(bf16[128,768]{1,0:T(8,128)(2,1)S(1)} %bitcast.127, ...), custom_call_target="tpu_custom_call" | custom-call | bytes 3784704 | tf_op jit(solution)/shard_map/pallas_call | solution.py:364
  45.6 1.2 multiply_convert_fusion.2
  47.9 1.1 fusion.68
  50.0 1.9 select_reduce_fusion
  52.0 2.4 %fusion.1 = f32[2,1024]{1,0:T(2,128)S(1)} fusion(f32[2,1024,1024]{1,2,0:T(8,128)S(1)} %get-tuple-element.108, f32[2,1024]{1,0:T(2,128)S(1)} %get-tuple-element.107, pred[1024,1024]{0,1:T(8,128)(4,1)S(1)} %broadcast_compare_fusion), kind=kLoop, calls=%fused_computation.5 | loop fusion | flops 10483712 | bytes 9453568 | tf_op jit(solution)/shard_map/reduce_sum | solution.py:455
  55.3 2.9 %fusion.102 = (bf16[2,1024,64]{1,2,0:T(8,128)(2,1)S(1)}, f32[2,1024,64]{1,2,0:T(8,128)S(1)}) fusion(f32[2,1024]{1,0:T(2,128)S(1)} %fusion.1, f32[2,1024,1024]{1,2,0:T(8,128)S(1)} %get-tuple-element.108, f32[2,1024]{1,0:T(2,128)S(1)} %get-tuple-element.107, pred[1024,1024]{0,1:T(8,128)(4,1)S(1)} %broadcast_compare_fusion, ...), kind=kOutput, calls=%fused_computation.201 | convolution fusion | flops 279838720 | bytes 10502145 | tf_op jit(solution)/shard_map/hqk,hke->hqe/dot_general | solution.py:456
  58.8 18.9 %shard_map.153 = (f32[128,768]{1,0:T(8,128)S(1)}, bf16[4,192,384]{2,1,0:T(8,128)(2,1)S(1)}) custom-call(bf16[8,128,768]{2,1,0:T(8,128)(2,1)S(1)} %bitcast.126, bf16[192,384]{1,0:T(8,128)(2,1)S(1)} %copy-done.11), custom_call_target="tpu_custom_call" | custom-call | bytes 7028736 | tf_op jit(solution)/shard_map/pallas_call | solution.py:364
  78.8 15.4 %shard_map.154 = (bf16[8,128,768]{2,1,0:T(8,128)(2,1)S(1)}, bf16[4,48,768]{2,1,0:T(8,128)(2,1)S(1)}) custom-call(bf16[128,768]{1,0:T(8,128)(2,1)S(1)} %multiply_convert_fusion.5.refs_0_, bf16[48,768]{1,0:T(8,128)(2,1)S(1)} %copy-done.13), custom_call_target="tpu_custom_call" | custom-call | bytes 1277952 | tf_op jit(solution)/shard_map/pallas_call | solution.py:364
  95.1 1.7 multiply_convert_fusion.3
  98.2 1.0 convolution_convert_fusion.4
  100.9 22.6 %shard_map.155 = (f32[128,768]{1,0:T(8,128)S(1)}, f32[128,768]{1,0:T(8,128)S(1)}, bf16[192,384]{1,0:T(8,128)(2,1)S(1)}) custom-call(bf16[8,128,768]{2,1,0:T(8,128)(2,1)S(1)} %bitcast.130, bf16[8,128,768]{2,1,0:T(8,128)(2,1)S(1)} %bitcast.123, bf16[4,192,384]{2,1,0:T(8,128)(2,1)S(1)} %bitcast.141), custom_call_target="tpu_custom_call" | custom-call | bytes 15187968 | tf_op jit(solution)/shard_map/pallas_call | solution.py:364
  124.7 14.9 %shard_map.156 = (bf16[8,128,768]{2,1,0:T(8,128)(2,1)S(1)}, bf16[8,16,768]{2,1,0:T(8,128)(2,1)S(1)}, bf16[48,768]{1,0:T(8,128)(2,1)S(1)}) custom-call(bf16[128,768]{1,0:T(8,128)(2,1)S(1)} %get-tuple-element.59.refs_0_, bf16[16,768]{1,0:T(8,128)(2,1)S(1)} %pad.28.refs_1_, bf16[4,48,768]{2,1,0:T(8,128)(2,1)S(1)} %bitcast.134), custom_call_target="tpu_custom_call" | custom-call | bytes 2359296 | tf_op jit(solution)/shard_map/pallas_call | solution.py:364
  141.7 5.6 %fusion.3 = bf16[2,1024,64]{1,2,0:T(8,128)(2,1)S(1)} fusion(f32[2,1024,1024]{1,2,0:T(8,128)} %copy-done.20, f32[2,1024]{1,0:T(2,128)} %log_add_fusion, pred[1024,1024]{0,1:T(8,128)(4,1)S(1)} %copy-done.22, bf16[1,1024,64]{1,2,0:T(8,128)(2,1)S(1)} %get-tuple-element.97, bf16[1,1024,64]{1,2,0:T(8,128)(2,1)S(1)} %get-tuple-element.96), kind=kOutput, calls=%fused_computation.7 | convolution fusion | flops 276955136 | bytes 9969664 | tf_op jit(solution)/shard_map/hqk,hqe->hke/dot_general | solution.py:533
  147.4 5.3 %multiply_convert_fusion = bf16[2,1024,1024]{1,2,0:T(8,128)(2,1)S(1)} fusion(f32[2,1024,1024]{1,2,0:T(8,128)} %copy-done.20, f32[2,1024]{1,0:T(2,128)S(1)} %multiply_reduce_fusion.2, f32[2,1024]{1,0:T(2,128)S(1)} %copy-done.39, pred[1024,1024]{0,1:T(8,128)(4,1)S(1)} %copy-done.22, bf16[1,1024,64]{1,2,0:T(8,128)(2,1)S(1)} %copy-done.37, ...), kind=kOutput, calls=%fused_computation | convolution fusion | flops 281280512 | bytes 14172160 | tf_op jit(solution)/shard_map/hqe,hke->hqk/dot_general | solution.py:525
  152.7 1.4 convolution_multiply_fusion.1
  158.1 1.4 multiply_reduce_fusion
  159.5 1.9 convolution_convert_fusion.3
  161.6 1.1 copy-done.9
  162.6 41.9 %shard_map.157 = (f32[128,768]{1,0:T(8,128)S(1)}, f32[192,2304]{1,0:T(8,128)S(1)}, f32[192,2304]{1,0:T(8,128)S(1)}, bf16[8,128,768]{2,1,0:T(8,128)(2,1)S(1)}, bf...) custom-call(bf16[8,128,768]{2,1,0:T(8,128)(2,1)S(1)} %bitcast.133, bf16[192,384]{1,0:T(8,128)(2,1)S(1)} %copy-done.15, ...), custom_call_target="tpu_custom_call" | custom-call | bytes 10878976 | tf_op jit(solution)/shard_map/pallas_call | solution.py:364
  206.8 1.9 fusion.31
  208.7 1.2 copy.48
  209.9 1.2 copy.49
  (168 shorter events, 32.9 us)
Async XLA Ops:
  0.6 4.9 %copy-start = (bf16[288,768]{1,0:T(8,128)(2,1)S(1)}, bf16[288,768]{1,0:T(8,128)(2,1)}, u32[]{:S(2)}) copy-start(bf16[288,768]{1,0:T(8,128)(2,1)} %param.14) | copy-start | bytes 1327108
  0.7 8.5 %copy-start.23 = (bf16[192,2304]{1,0:T(8,128)(2,1)S(1)}, bf16[192,2304]{1,0:T(8,128)(2,1)}, u32[]{:S(2)}) copy-start(bf16[192,2304]{1,0:T(8,128)(2,1)} %param.13) | copy-start | bytes 2654212
  2.5 8.2 %copy-start.2 = (bf16[1,128,768]{2,1,0:T(8,128)(2,1)S(1)}, bf16[1,128,768]{2,1,0:T(8,128)(2,1)}, u32[]{:S(2)}) copy-start(bf16[1,128,768]{2,1,0:T(8,128)(2,1)} %param.9) | copy-start | bytes 589828
  2.5 8.2 %copy-start.3 = (bf16[1,128,768]{2,1,0:T(8,128)(2,1)S(1)}, bf16[1,128,768]{2,1,0:T(8,128)(2,1)}, u32[]{:S(2)}) copy-start(bf16[1,128,768]{2,1,0:T(8,128)(2,1)} %param.17) | copy-start | bytes 589828
  45.6 9.6 %copy-start.21 = (pred[1024,1024]{0,1:T(8,128)(4,1)}, pred[1024,1024]{0,1:T(8,128)(4,1)S(1)}, u32[]{:S(2)}) copy-start(pred[1024,1024]{0,1:T(8,128)(4,1)S(1)} %broadcast_compare_fusion) | copy-start | bytes 3145732
  47.8 7.5 %copy-start.34 = (bf16[1,1024,64]{1,2,0:T(8,128)(2,1)}, bf16[1,1024,64]{1,2,0:T(8,128)(2,1)S(1)}, u32[]{:S(2)}) copy-start(bf16[1,1024,64]{1,2,0:T(8,128)(2,1)S(1)} %get-tuple-element.81) | copy-start | bytes 393220
  47.8 7.4 %copy-start.36 = (bf16[1,1024,64]{1,2,0:T(8,128)(2,1)}, bf16[1,1024,64]{1,2,0:T(8,128)(2,1)S(1)}, u32[]{:S(2)}) copy-start(bf16[1,1024,64]{1,2,0:T(8,128)(2,1)S(1)} %get-tuple-element.82) | copy-start | bytes 393220
  49.0 3.0 %copy-start.24 = (bf16[1,1024,64]{1,2,0:T(8,128)(2,1)}, bf16[1,1024,64]{1,2,0:T(8,128)(2,1)S(1)}, u32[]{:S(2)}) copy-start(bf16[1,1024,64]{1,2,0:T(8,128)(2,1)S(1)} %get-tuple-element.71) | copy-start | bytes 393220
  49.0 3.0 %copy-start.26 = (bf16[1,1024,64]{1,2,0:T(8,128)(2,1)}, bf16[1,1024,64]{1,2,0:T(8,128)(2,1)S(1)}, u32[]{:S(2)}) copy-start(bf16[1,1024,64]{1,2,0:T(8,128)(2,1)S(1)} %get-tuple-element.69) | copy-start | bytes 393220
  49.0 3.0 %copy-start.28 = (bf16[1,1024,64]{1,2,0:T(8,128)(2,1)}, bf16[1,1024,64]{1,2,0:T(8,128)(2,1)S(1)}, u32[]{:S(2)}) copy-start(bf16[1,1024,64]{1,2,0:T(8,128)(2,1)S(1)} %get-tuple-element.70) | copy-start | bytes 393220
  52.0 6.1 %copy-start.20 = (f32[2,1024,1024]{1,2,0:T(8,128)}, f32[2,1024,1024]{1,2,0:T(8,128)S(1)}, u32[]{:S(2)}) copy-start(f32[2,1024,1024]{1,2,0:T(8,128)S(1)} %get-tuple-element.108) | copy-start | bytes 25165828
  55.2 3.6 %copy-start.11 = (bf16[192,384]{1,0:T(8,128)(2,1)S(1)}, bf16[192,384]{1,0:T(8,128)(2,1)}, u32[]{:S(2)}) copy-start(bf16[192,384]{1,0:T(8,128)(2,1)} %copy.24.refs_1_) | copy-start | bytes 442372
  58.1 19.6 %copy-start.40 = (f32[128]{0:T(128)S(1)}, f32[128]{0:T(128)}, u32[]{:S(2)}) copy-start(f32[128]{0:T(128)} %broadcast_multiply_fusion.4) | copy-start | bytes 1540
  58.1 20.7 %copy-start.13 = (bf16[48,768]{1,0:T(8,128)(2,1)S(1)}, bf16[48,768]{1,0:T(8,128)(2,1)}, u32[]{:S(2)}) copy-start(bf16[48,768]{1,0:T(8,128)(2,1)} %pad.27.refs_1_) | copy-start | bytes 221188
  123.4 17.5 %copy-start.14 = (bf16[192,384]{1,0:T(8,128)(2,1)}, bf16[192,384]{1,0:T(8,128)(2,1)S(1)}, u32[]{:S(2)}) copy-start(bf16[192,384]{1,0:T(8,128)(2,1)S(1)} %get-tuple-element.43.refs_1_) | copy-start | bytes 442372
  124.7 17.0 %copy-start.22 = (pred[1024,1024]{0,1:T(8,128)(4,1)S(1)}, pred[1024,1024]{0,1:T(8,128)(4,1)}, u32[]{:S(2)}) copy-start(pred[1024,1024]{0,1:T(8,128)(4,1)} %copy-done.21) | copy-start | bytes 3145732
  141.7 5.6 %copy-start.35 = (bf16[1,1024,64]{1,2,0:T(8,128)(2,1)S(1)}, bf16[1,1024,64]{1,2,0:T(8,128)(2,1)}, u32[]{:S(2)}) copy-start(bf16[1,1024,64]{1,2,0:T(8,128)(2,1)} %copy-done.34) | copy-start | bytes 393220
  141.7 5.6 %copy-start.37 = (bf16[1,1024,64]{1,2,0:T(8,128)(2,1)S(1)}, bf16[1,1024,64]{1,2,0:T(8,128)(2,1)}, u32[]{:S(2)}) copy-start(bf16[1,1024,64]{1,2,0:T(8,128)(2,1)} %copy-done.36) | copy-start | bytes 393220
  141.7 5.7 %copy-start.39 = (f32[2,1024]{1,0:T(2,128)S(1)}, f32[2,1024]{1,0:T(2,128)}, u32[]{:S(2)}) copy-start(f32[2,1024]{1,0:T(2,128)} %log_add_fusion) | copy-start | bytes 24580
  147.3 5.4 %copy-start.27 = (bf16[1,1024,64]{1,2,0:T(8,128)(2,1)S(1)}, bf16[1,1024,64]{1,2,0:T(8,128)(2,1)}, u32[]{:S(2)}) copy-start(bf16[1,1024,64]{1,2,0:T(8,128)(2,1)} %copy-done.26) | copy-start | bytes 393220
  147.3 5.4 %copy-start.29 = (bf16[1,1024,64]{1,2,0:T(8,128)(2,1)S(1)}, bf16[1,1024,64]{1,2,0:T(8,128)(2,1)}, u32[]{:S(2)}) copy-start(bf16[1,1024,64]{1,2,0:T(8,128)(2,1)} %copy-done.28) | copy-start | bytes 393220
  161.4 45.2 %copy-start.41 = (f32[128]{0:T(128)S(1)}, f32[128]{0:T(128)}, u32[]{:S(2)}) copy-start(f32[128]{0:T(128)} %broadcast_multiply_fusion.4) | copy-start | bytes 1540
  161.4 45.2 %copy-start.44 = (f32[128]{0:T(128)S(1)}, f32[128]{0:T(128)}, u32[]{:S(2)}) copy-start(f32[128]{0:T(128)} %add_rsqrt_fusion.1) | copy-start | bytes 1540
  208.7 3.3 %copy-start.1 = (bf16[288,768]{1,0:T(8,128)(2,1)S(1)}, bf16[288,768]{1,0:T(8,128)(2,1)}, u32[]{:S(2)}) copy-start(bf16[288,768]{1,0:T(8,128)(2,1)} %param.14) | copy-start | bytes 1327108
  (22 other events, 33.2 us)

commit v4 on v3

--- a/solution.py
+++ b/solution.py
@@ -2,6 +2,7 @@
 
 import jax
 import jax.numpy as jnp
+import numpy as np
 from jax import lax
 from jax.experimental import pallas as pl
 from jax.experimental.pallas import tpu as pltpu
@@ -42,11 +43,12 @@
 
 
 def rope_tables(row_count, head_size, heads):
-    position = jnp.arange(row_count, dtype=jnp.int32).astype(F32)
-    frequency = ROPE_THETA ** (-jnp.arange(0, head_size, 2, dtype=F32) / head_size)
+    position = np.arange(row_count).astype(np.float32)
+    power = -np.arange(0, head_size, 2).astype(np.float32) / np.float32(head_size)
+    frequency = (ROPE_THETA ** power.astype(np.float64)).astype(np.float32)
     angles = position[:, None] * frequency[None, :]
-    angles = jnp.concatenate([angles, angles], axis=-1)
-    return jnp.cos(angles), jnp.sin(angles)
+    angles = np.concatenate([angles, angles], axis=-1).astype(np.float64)
+    return np.cos(angles).astype(np.float32), np.sin(angles).astype(np.float32)
 
 
 def rotary(values, cosines, sines):
@@ -444,7 +446,7 @@
         values = jnp.stack([head_of(2, h) for h in range(per)]).astype(BF)
         chunk = min(tokens, 1024)
         pieces = tokens // chunk
-        attention, log_total = [], []
+        attention, kept, inverses = [], [], []
         for c in range(pieces):
             part = slice(c * chunk, (c + 1) * chunk)
             scores = jnp.einsum("hqe,hke->hqk", queries[:, part], keys, preferred_element_type=F32) * scale
@@ -453,9 +455,10 @@
             highest = jnp.max(scores, axis=-1, keepdims=True)
             weights = jnp.where(allowed, jnp.exp(scores - highest), 0.0)
             total = jnp.sum(weights, axis=-1, keepdims=True)
-            summed = jnp.einsum("hqk,hke->hqe", weights.astype(BF), values, preferred_element_type=F32)
-            attention.append(summed / total)
-            log_total.append(highest + jnp.log(total))
+            kept.append(weights.astype(BF))
+            inverses.append(1.0 / total)
+            summed = jnp.einsum("hqk,hke->hqe", kept[c], values, preferred_element_type=F32)
+            attention.append(summed * inverses[c])
         attention_all = jnp.concatenate(attention, axis=1)
         attention_all = jnp.where(valid, attention_all, 0.0)
         attended = jnp.concatenate([attention_all[h] for h in range(per)], axis=1).astype(BF)
@@ -517,13 +520,10 @@
         grad_queries, grad_keys, grad_values = [], 0.0, 0.0
         for c in range(pieces):
             part = slice(c * chunk, (c + 1) * chunk)
-            scores = jnp.einsum("hqe,hke->hqk", queries[:, part], keys, preferred_element_type=F32) * scale
-            allowed = (ids[part][:, None] == ids[None, :])[None]
-            probs = jnp.where(allowed, jnp.exp(scores - log_total[c]), 0.0)
             grad_part = grad_heads[:, part]
             products = jnp.sum(grad_part.astype(F32) * attention_all[:, part], axis=-1, keepdims=True)
             grad_probs = jnp.einsum("hqe,hke->hqk", grad_part, values, preferred_element_type=F32)
-            grad_scores = (probs * (grad_probs - products)).astype(BF)
+            grad_scores = (kept[c].astype(F32) * ((grad_probs - products) * inverses[c])).astype(BF)
             grad_queries.append(
                 scale * jnp.einsum("hqk,hke->hqe", grad_scores, keys, preferred_element_type=F32)
             )
@@ -531,7 +531,10 @@
                 "hqk,hqe->hke", grad_scores, queries[:, part], preferred_element_type=F32
             )
             grad_values += jnp.einsum(
-                "hqk,hqe->hke", probs.astype(BF), grad_part, preferred_element_type=F32
+                "hqk,hqe->hke",
+                kept[c],
+                (grad_part.astype(F32) * inverses[c]).astype(BF),
+                preferred_element_type=F32,
             )
         grad_queries = jnp.concatenate(grad_queries, axis=1)
         grad_projected = jnp.concatenate(

time: 212 us -> 202 us (0.953)
  other arithmetic: 24.6 us -> 15.2 us
    sub x0 -> x1, matrix products: none -> 8.3 us  [local(): weights = jnp.where(allowed, jnp.exp(scores - highest), 0.0)]
    dot_general x1, matrix products: 5.32 us -> 1.54 us  [local(): jnp.einsum('hqe,hke->hqk', grad_part, values, preferred_element_type=F32)]
    dot_general x3 -> x2, matrix products: 10.4 us -> 6.91 us  [the longest x1 3.73 us: local(): jnp.einsum('hqk,hqe->hke', kept[c], (grad_part.astype(F32) * inverses[c])...]
    unnamed x97 -> x63, local copies, waits for them, and re-layouts: 9.11 us -> 6.46 us
    reduce_sum x1 -> x0, other arithmetic: 2.44 us -> none  [local(): total = jnp.sum(weights, axis=-1, keepdims=True)]
where the time goes in v4:
time: 202 us
  Pallas kernels  141 us (70%)
  matrix products  30.2 us (15%)
  other arithmetic  15.2 us (8%)
  local copies, waits for them, and re-layouts  14.2 us (7%)
    pallas_call x6, Pallas kernels, exchange(): pl.pallas_call(kernel, out_shape=outs, in_specs=[vmem] * len(tasks), out_...  141 us
    sub x1, matrix products, local(): weights = jnp.where(allowed, jnp.exp(scores - highest), 0.0)  8.3 us
    unnamed x63, local copies, waits for them, and re-layouts  6.46 us
    dot_general x4, matrix products, dot_t(): lax.dot_general(a, b, (((1,), (1,)), ((), ())), preferred_element_type=F32)  5.34 us

profile of v4, /device:TPU:0, one launch (start us, length us, event | category | flops | bytes accessed | tf_op | source)
XLA Modules:
  0.0 202.0 jit_solution(11000282988472964662)
XLA Ops:
  1.4 1.0 convert_reduce_fusion.1
  4.5 2.2 %reshape.244 = bf16[192,3,768]{2,1,0:T(4,128)(2,1)S(1)} reshape(bf16[192,2304]{1,0:T(8,128)(2,1)} %param.13) | data formatting | bytes 1769472 | tf_op jit(solution)/shard_map/reshape | solution.py:406
  6.8 1.6 copy.38
  8.6 1.0 copy-done.6
  9.6 27.4 %shard_map.170 = (bf16[8,128,768]{2,1,0:T(8,128)(2,1)S(1)}, bf16[4,192,384]{2,1,0:T(8,128)(2,1)S(1)}, bf16[4,16,192]{2,1,0:T(8,128)(2,1)S(1)}, bf16[8,16,128]{2,...) custom-call(bf16[128,768]{1,0:T(8,128)(2,1)S(1)} %bitcast.121, ...), custom_call_target="tpu_custom_call" | custom-call | bytes 3784704 | tf_op jit(solution)/shard_map/pallas_call | solution.py:366
  39.5 1.6 broadcast_compare_fusion
  44.6 8.3 %fusion.83 = (f32[2,1024]{1,0:T(2,128)S(1)}, bf16[2,1024,1024]{1,2,0:T(8,128)(2,1)}) fusion(pred[1024,1024]{0,1:T(8,128)(4,1)} %broadcast_compare_fusion, bf16[1,1024,64]{1,2,0:T(8,128)(2,1)} %get-tuple-element.72, bf16[1,1024,64]{1,2,0:T(8,128)(2,1)S(1)} %get-tuple-element.71, bf16[1,1024,64]{1,2,0:T(8,128)(2,1)} %get-tuple-element.70, ...), kind=kOutput, calls=%fused_computation.189 | convolution fusion | flops 281281536 | bytes 5775360 | tf_op jit(solution)/shard_map/sub | solution.py:456
  52.9 3.2 %fusion.85 = (bf16[2,1024,64]{1,2,0:T(8,128)(2,1)S(1)}, f32[2,1024,64]{1,2,0:T(8,128)S(1)}) fusion(f32[2,1024]{1,0:T(2,128)S(1)} %broadcast_divide_fusion, bf16[2,1024,1024]{1,2,0:T(8,128)(2,1)} %get-tuple-element.109, bf16[1,1024,64]{1,2,0:T(8,128)(2,1)} %get-tuple-element.87, bf16[1,1024,64]{1,2,0:T(8,128)(2,1)} %get-tuple-element.86, pred[]{:T(512)S(6)} %lt.13), kind=kOutput, calls=%fused_computation.191 | convolution fusion | flops 269352960 | bytes 5251073 | tf_op jit(solution)/shard_map/hqk,hke->hqe/dot_general | solution.py:460
  56.7 18.9 %shard_map.171 = (f32[128,768]{1,0:T(8,128)S(1)}, bf16[4,192,384]{2,1,0:T(8,128)(2,1)S(1)}) custom-call(bf16[8,128,768]{2,1,0:T(8,128)(2,1)S(1)} %bitcast.120, bf16[192,384]{1,0:T(8,128)(2,1)S(1)} %copy.26.refs_1_), custom_call_target="tpu_custom_call" | custom-call | bytes 7028736 | tf_op jit(solution)/shard_map/pallas_call | solution.py:366
  76.8 15.4 %shard_map.172 = (bf16[8,128,768]{2,1,0:T(8,128)(2,1)S(1)}, bf16[4,48,768]{2,1,0:T(8,128)(2,1)S(1)}) custom-call(bf16[128,768]{1,0:T(8,128)(2,1)S(1)} %multiply_convert_fusion.5.refs_0_, bf16[48,768]{1,0:T(8,128)(2,1)S(1)} %copy-done.7), custom_call_target="tpu_custom_call" | custom-call | bytes 1277952 | tf_op jit(solution)/shard_map/pallas_call | solution.py:366
  93.0 1.9 multiply_convert_fusion.3
  96.4 1.0 convolution_convert_fusion.4
  97.4 1.0 convolution_convert_fusion
  99.0 22.6 %shard_map.173 = (f32[128,768]{1,0:T(8,128)S(1)}, f32[128,768]{1,0:T(8,128)S(1)}, bf16[192,384]{1,0:T(8,128)(2,1)S(1)}) custom-call(bf16[8,128,768]{2,1,0:T(8,128)(2,1)S(1)} %bitcast.124, bf16[8,128,768]{2,1,0:T(8,128)(2,1)S(1)} %bitcast.117, bf16[4,192,384]{2,1,0:T(8,128)(2,1)S(1)} %bitcast.135), custom_call_target="tpu_custom_call" | custom-call | bytes 15187968 | tf_op jit(solution)/shard_map/pallas_call | solution.py:366
  121.9 1.0 fusion.76
  122.9 14.9 %shard_map.174 = (bf16[8,128,768]{2,1,0:T(8,128)(2,1)S(1)}, bf16[8,16,768]{2,1,0:T(8,128)(2,1)S(1)}, bf16[48,768]{1,0:T(8,128)(2,1)S(1)}) custom-call(bf16[128,768]{1,0:T(8,128)(2,1)S(1)} %get-tuple-element.59.refs_0_, bf16[16,768]{1,0:T(8,128)(2,1)S(1)} %pad.28.refs_1_, bf16[4,48,768]{2,1,0:T(8,128)(2,1)S(1)} %bitcast.128), custom_call_target="tpu_custom_call" | custom-call | bytes 2359296 | tf_op jit(solution)/shard_map/pallas_call | solution.py:366
  139.7 3.7 %fusion.29 = bf16[2,1024,64]{1,2,0:T(8,128)(2,1)S(1)} fusion(f32[2,1024]{1,0:T(2,128)S(1)} %broadcast_divide_fusion, bf16[1,1024,64]{1,2,0:T(8,128)(2,1)S(1)} %get-tuple-element.100, bf16[1,1024,64]{1,2,0:T(8,128)(2,1)S(1)} %get-tuple-element.99, bf16[2,1024,1024]{1,2,0:T(8,128)(2,1)} %get-tuple-element.109), kind=kOutput, calls=%fused_computation.79 | convolution fusion | flops 268959744 | bytes 4726784 | tf_op jit(solution)/shard_map/hqk,hqe->hke/dot_general | solution.py:533
  143.5 1.5 multiply_convert_fusion
  145.0 1.4 convolution_multiply_fusion.2
  149.3 2.8 %multiply_reduce_fusion = (bf16[768]{0:T(1024)(128)(2,1)S(1)}, bf16[1024,768]{1,0:T(8,128)(2,1)}, bf16[1024,768]{1,0:T(8,128)(2,1)S(1)}) fusion(bf16[8,128,768]{2,1,0:T(8,128)(2,1)S(1)} %get-tuple-element.31, f32[1024]{0:T(1024)S(1)} %copy-done.28, f32[1024]{0:T(1024)S(1)} %copy-done.27, f32[768]{0:T(1024)S(1)} %copy-done.22, ...), kind=kOutput, calls=%fused_computation.10 | convolution fusion | flops 610663680 | bytes 6107649 | tf_op jit(solution)/shard_map/dot_general | solution.py:24
  152.1 1.0 convolution_convert_fusion.3
  153.5 41.9 %shard_map.175 = (f32[128,768]{1,0:T(8,128)S(1)}, f32[192,2304]{1,0:T(8,128)S(1)}, f32[192,2304]{1,0:T(8,128)S(1)}, bf16[8,128,768]{2,1,0:T(8,128)(2,1)S(1)}, bf...) custom-call(bf16[8,128,768]{2,1,0:T(8,128)(2,1)S(1)} %bitcast.127, bf16[192,384]{1,0:T(8,128)(2,1)S(1)} %get-tuple-element.43.refs_1_, ...), custom_call_target="tpu_custom_call" | custom-call | bytes 10878976 | tf_op jit(solution)/shard_map/pallas_call | solution.py:366
  198.6 1.2 copy.50
  199.9 1.2 copy.51
  (129 shorter events, 22.9 us)
Async XLA Ops:
  0.6 3.1 %copy-start = (bf16[288,768]{1,0:T(8,128)(2,1)S(1)}, bf16[288,768]{1,0:T(8,128)(2,1)}, u32[]{:S(2)}) copy-start(bf16[288,768]{1,0:T(8,128)(2,1)} %param.16) | copy-start | bytes 1327108
  2.4 73.2 %copy-start.24 = (f32[128]{0:T(128)}, f32[128]{0:T(128)S(1)}, u32[]{:S(2)}) copy-start(f32[128]{0:T(128)S(1)} %broadcast_multiply_fusion.3) | copy-start | bytes 1540
  6.8 1.8 copy-start.1
  6.8 1.8 copy-start.5
  8.6 1.0 copy-start.6
  37.0 1.7 copy-start.2
  39.5 2.2 %copy-start.21 = (f32[768]{0:T(1024)}, f32[768]{0:T(1024)S(1)}, u32[]{:S(2)}) copy-start(f32[768]{0:T(1024)S(1)} %reshape.263) | copy-start | bytes 9220
  42.5 1.0 copy-start.19
  42.5 1.1 copy-start.20
  44.6 8.3 %copy-start.11 = (bf16[1,1024,64]{1,2,0:T(8,128)(2,1)}, bf16[1,1024,64]{1,2,0:T(8,128)(2,1)S(1)}, u32[]{:S(2)}) copy-start(bf16[1,1024,64]{1,2,0:T(8,128)(2,1)S(1)} %get-tuple-element.71) | copy-start | bytes 393220
  56.7 20.1 %copy-start.7 = (bf16[48,768]{1,0:T(8,128)(2,1)S(1)}, bf16[48,768]{1,0:T(8,128)(2,1)}, u32[]{:S(2)}) copy-start(bf16[48,768]{1,0:T(8,128)(2,1)} %pad.27.refs_1_) | copy-start | bytes 221188
  93.0 1.9 copy-start.3
  139.7 3.7 %copy-start.8 = (bf16[2,1024,1024]{1,2,0:T(8,128)(2,1)S(1)}, bf16[2,1024,1024]{1,2,0:T(8,128)(2,1)}, u32[]{:S(2)}) copy-start(bf16[2,1024,1024]{1,2,0:T(8,128)(2,1)} %get-tuple-element.109) | copy-start | bytes 12582916
  139.7 3.7 %copy-start.16 = (bf16[1,1024,64]{1,2,0:T(8,128)(2,1)S(1)}, bf16[1,1024,64]{1,2,0:T(8,128)(2,1)}, u32[]{:S(2)}) copy-start(bf16[1,1024,64]{1,2,0:T(8,128)(2,1)} %get-tuple-element.86) | copy-start | bytes 393220
  139.7 3.8 %copy-start.17 = (bf16[1,1024,64]{1,2,0:T(8,128)(2,1)S(1)}, bf16[1,1024,64]{1,2,0:T(8,128)(2,1)}, u32[]{:S(2)}) copy-start(bf16[1,1024,64]{1,2,0:T(8,128)(2,1)} %get-tuple-element.87) | copy-start | bytes 393220
  143.4 1.6 copy-start.14
  143.5 1.6 copy-start.15
  145.0 1.4 copy-start.12
  145.0 1.4 copy-start.13
  152.1 1.1 copy-start.23
  152.1 1.4 copy-start.4
  153.5 43.9 %copy-start.25 = (f32[128]{0:T(128)S(1)}, f32[128]{0:T(128)}, u32[]{:S(2)}) copy-start(f32[128]{0:T(128)} %copy-done.24) | copy-start | bytes 1540
  153.5 43.9 %copy-start.26 = (f32[128]{0:T(128)S(1)}, f32[128]{0:T(128)}, u32[]{:S(2)}) copy-start(f32[128]{0:T(128)} %get-tuple-element.115) | copy-start | bytes 1540
  153.5 44.2 %copy-start.10 = (f32[128,768]{1,0:T(8,128)S(1)}, f32[128,768]{1,0:T(8,128)}, u32[]{:S(2)}) copy-start(f32[128,768]{1,0:T(8,128)} %get-tuple-element.60) | copy-start | bytes 1179652
  (5 other events, 4.0 us)
